TPU v7x, 32 devices: a whole 2x2x4 slice. The times are simulated.
32 devices in a mesh: blk: 32 (over z, y, x, core).
Axes of the slice: x: 2, y: 2, z: 4, core: 2. Of those that a mesh axis runs over, the one named last changes fastest.
Arguments:
- f_coarse: float32 [64, 27, 512], P('blk'), as said below
- f_mid: float32 [128, 27, 512], P('blk'), as said below
- f_fine: float32 [256, 27, 512], P('blk'), as said below
- solid_coarse: float32 [64, 512], P('blk'), may hold values from 0 to 0.7
- solid_mid: float32 [128, 512], P('blk'), may hold values from 0 to 0.7
- solid_fine: float32 [256, 512], P('blk'), may hold values from 0 to 0.7
- rates: float32 [3, 27], replicated, may hold values from 0.6 to 1.8
- faces_coarse: int32 [64, 6], P('blk'), may hold values from -1 to 63, as said below
- faces_mid: int32 [128, 6], P('blk'), may hold values from -1 to 127, as said below
- faces_fine: int32 [256, 6], P('blk'), may hold values from -1 to 255, as said below
- explode_mid: int32 [128, 2], P('blk'), may hold values from -1 to 63, as said below
- explode_fine: int32 [256, 2], P('blk'), may hold values from -1 to 127, as said below
- coalesce_coarse: int32 [64, 8], P('blk'), may hold values from -1 to 127, as said below
- coalesce_mid: int32 [128, 8], P('blk'), may hold values from -1 to 255, as said below
Outputs:
- coarse_out: float32 [64, 27, 512], P('blk')
- mid_out: float32 [128, 27, 512], P('blk')
- fine_out: float32 [256, 27, 512], P('blk')
Inputs may be any that keep to these rules, and one draw needn't show every extreme that they name: `faces_coarse`: block g of a level with 2 blocks a group lies in group g // 2; every named block lies in the same group as g or in one of the two beside it, and some block names the group below and some the group above. `faces_mid`: likewise with 4 blocks a group. `faces_fine`: likewise with 8 blocks a group. `explode_mid`: column 0 is a coarse block or -1, lying in group q // 4 of its own level counted in groups of 2 blocks, or one beside it; column 1 is an octant 0 to 7. `explode_fine`: column 0 is a middle-level block or -1, in the group q // 8 counted in groups of 4 blocks, or one beside it; column 1 is an octant 0 to 7. `coalesce_coarse`: each entry is a middle-level block or -1, in group p // 2 counted in groups of 4 blocks, or one beside it. `coalesce_mid`: each entry is a fine block or -1, in group p // 4 counted in groups of 8 blocks, or one beside it. `f_coarse`: positive in every entry. `f_mid`: positive in every entry. `f_fine`: positive in every entry.
All inputs are finite; a program needn't handle non-finite values.
Results may differ from a plain program's by a relative error of at most 0.0001.
Values sent between devices are 32-bit elements; how exact they have to be, the bound alone decides.
A program may use at most 512 MiB of HBM per device.

v0:
```python
import jax
import jax.numpy as jnp
from jax import lax
from jax.sharding import PartitionSpec as P

C = 8


HIGH = lax.Precision.HIGHEST
V_ROWS = ((1.0, 1.0, 1.0), (-1.0, 0.0, 1.0), (1.0, 0.0, 1.0))
V_BACK = ((0.0, -0.5, 0.5), (1.0, 0.0, -1.0), (0.0, 0.5, 0.5))


def padded(array, sides, width):
    for axis, dim in sides:
        peers, length = (lax.axis_size(axis), array.shape[dim])
        up = [(i, (i + 1) % peers) for i in range(peers - 1)]
        down = [(j, i) for i, j in up]
        last = lax.slice_in_dim(array, length - width, length, axis=dim)
        first = lax.slice_in_dim(array, 0, width, axis=dim)
        before = lax.ppermute(last, axis, up)
        after = lax.ppermute(first, axis, down)
        array = jnp.concatenate([before, array, after], axis=dim)
    return array


def separable(field, table):
    matrix = jnp.asarray(table, jnp.float32)
    count = field.shape[0]
    cells = field.shape[-1]
    grid = field.reshape(count, 3, 3, 3, cells)
    grid = jnp.einsum("ai,nijks->najks", matrix, grid, precision=HIGH)
    grid = jnp.einsum("bj,najks->nabks", matrix, grid, precision=HIGH)
    grid = jnp.einsum("ck,nabks->nabcs", matrix, grid, precision=HIGH)
    return grid.reshape(count, 27, cells)


def moment_terms(speed):
    return jnp.stack([jnp.ones_like(speed), speed, 1.0 / 3.0 + speed * speed], axis=1)


def relax(moments, solid, rate):
    density = moments[:, 0]
    keep = (1.0 - solid) / density
    along_x = moment_terms(moments[:, 9] * keep)
    along_y = moment_terms(moments[:, 3] * keep)
    along_z = moment_terms(moments[:, 1] * keep)
    target = (
        density[:, None, None, None, :]
        * along_x[:, :, None, None, :]
        * along_y[:, None, :, None, :]
        * along_z[:, None, None, :, :]
    )
    target = target.reshape(moments.shape)
    return moments - rate[None, :, None] * (moments - target)


def collide(field, solid, rate):
    return separable(relax(separable(field, V_ROWS), solid, rate), V_BACK)


def split_velocity(field, axis, edge):
    grid = field.reshape((field.shape[0], 3, 3, 3, edge, edge, edge))
    return [lax.index_in_dim(grid, k, 1 + axis, keepdims=False) for k in range(3)]


def layer(part, index, axis):
    face = lax.index_in_dim(part, index, 3 + axis, keepdims=False)
    return face.reshape(face.shape[0], 9, -1)


def edges(field, axis, edge):
    minus, rest, plus = split_velocity(field, axis, edge)
    return (
        layer(plus, edge - 1, axis),
        layer(minus, 0, axis),
        layer(plus, 0, axis),
        layer(minus, edge - 1, axis),
    )


def stream(field, axis, edge, into_low, into_high):
    minus, rest, plus = split_velocity(field, axis, edge)
    spot = 3 + axis
    count = field.shape[0]
    low = jnp.expand_dims(into_low.reshape(count, 3, 3, edge, edge), spot)
    high = jnp.expand_dims(into_high.reshape(count, 3, 3, edge, edge), spot)
    plus = jnp.concatenate([low, lax.slice_in_dim(plus, 0, edge - 1, axis=spot)], axis=spot)
    minus = jnp.concatenate([lax.slice_in_dim(minus, 1, edge, axis=spot), high], axis=spot)
    grid = jnp.stack([minus, rest, plus], axis=1 + axis)
    return grid.reshape(count, 27, edge**3)


def settle(field, axis, edge, near, table, lowest, own_low, own_high):
    rows = near.shape[0]
    low_id = table[:, 2 * axis]
    high_id = table[:, 2 * axis + 1]
    low_at = jnp.clip(low_id - lowest, 0, rows - 1)
    high_at = jnp.clip(high_id - lowest, 0, rows - 1)
    into_low = jnp.where((low_id >= 0)[:, None, None], near[low_at, 0], own_low)
    into_high = jnp.where((high_id >= 0)[:, None, None], near[high_at, 1], own_high)
    return stream(field, axis, edge, into_low, into_high)


def octant_table(blocks, edge):
    half = edge // 2
    count = blocks.shape[0]
    grid = blocks.reshape(count, 27, 2, half, 2, half, 2, half).transpose(0, 2, 4, 6, 1, 3, 5, 7)
    return grid.reshape(count * 8, 27, half**3)


def lookup(table, wanted, lowest):
    blocks = table.shape[0] // 8
    slots = jnp.clip(jnp.maximum(wanted[:, 0], 0) - lowest, 0, blocks - 1) * 8 + wanted[:, 1]
    return table[slots]


def rim_mask(edge):
    line = jnp.arange(edge)
    side = (line == 0) | (line == edge - 1)
    return (side[:, None, None] | side[None, :, None] | side[None, None, :]).reshape(edge**3)


def explode(child, pieces, parent_id, edge):
    half = edge // 2
    count = child.shape[0]
    grid = pieces.reshape(count, 27, half, 1, half, 1, half, 1)
    grid = jnp.broadcast_to(grid, (count, 27, half, 2, half, 2, half, 2)).reshape(
        count, 27, edge**3
    )
    keep = (parent_id >= 0)[:, None, None] & rim_mask(edge)[None, None, :]
    return jnp.where(keep, grid, child)


def restrict(blocks, edge):
    half = edge // 2
    count = blocks.shape[0]
    grid = blocks.reshape(count, 27, half, 2, half, 2, half, 2)
    return (jnp.sum(grid, axis=(3, 5, 7)) * 0.125).reshape(count, 27, half**3)


def assemble(parent, means, child_id, edge):
    half = edge // 2
    count = parent.shape[0]
    grid = parent.reshape(count, 27, 2, half, 2, half, 2, half)
    parts = []
    for octant in range(8):
        old = grid[:, :, octant // 4, :, octant // 2 % 2, :, octant % 2, :]
        fresh = means[:, octant].reshape(count, 27, half, half, half)
        parts.append(jnp.where((child_id[:, octant] >= 0)[:, None, None, None, None], fresh, old))
    inner = [
        [jnp.stack([parts[ox * 4 + oy * 2], parts[ox * 4 + oy * 2 + 1]], axis=4) for oy in range(2)]
        for ox in range(2)
    ]
    middle = [jnp.stack(inner[ox], axis=3) for ox in range(2)]
    return jnp.stack(middle, axis=2).reshape(count, 27, edge**3)


def face_block(field, axis, edge):
    sent_high, sent_low, own_low, own_high = edges(field, axis, edge)
    count = field.shape[0]
    sent = jnp.stack([sent_high, sent_low], axis=1).reshape(1, count * 18, -1)
    return (sent, own_low, own_high)


def local(
    f_coarse,
    f_mid,
    f_fine,
    solid_coarse,
    solid_mid,
    solid_fine,
    rates,
    faces_coarse,
    faces_mid,
    faces_fine,
    explode_mid,
    explode_fine,
    coalesce_coarse,
    coalesce_mid,
):
    edge = C
    place = lax.axis_index("blk")
    n_coarse = f_coarse.shape[0]
    n_mid = f_mid.shape[0]
    n_fine = f_fine.shape[0]
    sent = jnp.concatenate(
        [f_coarse.reshape(1, n_coarse * 27, -1), f_mid.reshape(1, n_mid * 27, -1)], axis=1
    )
    beside_all = padded(sent, (("blk", 0),), 1)
    coarse_near = beside_all[:, : n_coarse * 27].reshape(3 * n_coarse, 27, -1)
    mid_near = beside_all[:, n_coarse * 27 :].reshape(3 * n_mid, 27, -1)
    pieces_mid = lookup(octant_table(coarse_near, edge), explode_mid, (place - 1) * n_coarse)
    pieces_fine = lookup(octant_table(mid_near, edge), explode_fine, (place - 1) * n_mid)
    mid_start = explode(f_mid, pieces_mid, explode_mid[:, 0], edge)
    fine_start = explode(f_fine, pieces_fine, explode_fine[:, 0], edge)
    fields = [f_coarse, mid_start, fine_start]
    solids = [solid_coarse, solid_mid, solid_fine]
    neighbours = [faces_coarse, faces_mid, faces_fine]
    substeps = [1, 2, 4]
    for level in range(3):
        field = fields[level]
        count = field.shape[0]
        for step in range(substeps[level]):
            field = collide(field, solids[level], rates[level])
            for axis in range(3):
                sent, own_low, own_high = face_block(field, axis, edge)
                near = padded(sent, (("blk", 0),), 1).reshape(3 * count, 2, 9, -1)
                field = settle(
                    field,
                    axis,
                    edge,
                    near,
                    neighbours[level],
                    (place - 1) * count,
                    own_low,
                    own_high,
                )
        fields[level] = field
    coarse, middle, fine_out = fields
    sent = jnp.concatenate(
        [
            restrict(middle, edge).reshape(1, n_mid * 27, -1),
            restrict(fine_out, edge).reshape(1, n_fine * 27, -1),
        ],
        axis=1,
    )
    near = padded(sent, (("blk", 0),), 1)
    mid_means = near[:, : n_mid * 27].reshape(3 * n_mid, 27, -1)
    fine_means = near[:, n_mid * 27 :].reshape(3 * n_fine, 27, -1)
    mid_at = jnp.clip(coalesce_coarse - (place - 1) * n_mid, 0, 3 * n_mid - 1)
    fine_at = jnp.clip(coalesce_mid - (place - 1) * n_fine, 0, 3 * n_fine - 1)
    coarse_out = assemble(coarse, mid_means[mid_at], coalesce_coarse, edge)
    mid_out = assemble(middle, fine_means[fine_at], coalesce_mid, edge)
    return (coarse_out, mid_out, fine_out)


def solution(mesh):
    placed = (
        P("blk", None, None),
        P("blk", None, None),
        P("blk", None, None),
        P("blk", None),
        P("blk", None),
        P("blk", None),
        P(),
        P("blk", None),
        P("blk", None),
        P("blk", None),
        P("blk", None),
        P("blk", None),
        P("blk", None),
        P("blk", None),
    )
    return jax.shard_map(
        local,
        mesh=mesh,
        in_specs=placed,
        out_specs=(P("blk", None, None), P("blk", None, None), P("blk", None, None)),
        check_vma=False,
    )
```

profile of v0, /device:TPU:23, one launch (start us, length us, event | category | flops | bytes accessed | tf_op | source)
XLA Modules:
  0.0 1073.8 jit_solution(17101017243219176459)
XLA Ops:
  6.2 4.8 collective-permute-start
  20.0 5.4 collective-permute-start.40
  52.4 5.4 collective-permute-start.42
  63.9 6.0 collective-permute-start.44
  83.8 3.7 reshape.1607
  87.5 3.9 fusion.186
  126.9 5.4 collective-permute-start.2
  144.8 10.5 bitcast_select_fusion
  164.6 5.4 reshape_reshape.57
  170.0 6.4 fusion.185
  192.7 5.7 collective-permute-start.14
  231.8 5.4 collective-permute-start.4
  253.8 3.6 pad_maximum_fusion
  274.4 5.8 collective-permute-start.6
  280.2 6.4 fusion.184
  329.1 5.4 collective-permute-start.8
  335.3 3.7 slice.1416
  341.6 5.4 collective-permute-start.16
  372.4 5.4 collective-permute-start.10
  414.4 5.4 collective-permute-start.18
  422.0 3.8 stack.613
  458.2 5.8 copy.1433
  469.2 3.9 stack.614
  474.8 5.8 copy.1430
  496.1 5.4 reshape_reshape.58
  501.5 6.4 fusion.182
  512.6 5.4 collective-permute-start.20
  541.0 5.4 collective-permute-start.22
  549.2 5.7 collective-permute-start.12
  594.9 5.7 collective-permute-start.24
  607.4 3.7 copy.1384
  613.2 3.6 stack.635
  629.6 5.8 copy.1467
  640.5 4.0 stack.636
  646.2 5.7 copy.1465
  667.5 5.4 reshape_reshape.59
  672.9 6.4 slice_bitcast_fusion.13
  692.3 5.4 collective-permute-start.26
  704.0 3.7 copy.1382
  748.7 5.7 collective-permute-start.28
  794.0 5.7 collective-permute-start.30
  810.0 4.8 copy.1502
  823.6 4.8 copy.1500
  841.3 5.4 reshape_reshape.60
  846.7 6.4 slice_bitcast_fusion.5
  866.3 5.4 collective-permute-start.32
  892.9 5.4 collective-permute-start.34
  900.7 12.0 %copy.1385 = f32[4,3,3,3,8,8,8]{0,6,5,4,3,2,1:T(8,128)} copy(f32[4,3,3,3,8,8,8]{6,5,4,0,2,1,3:T(8,128)S(1)} %pad_maximum_fusion.13) | data formatting | bytes 442368 | tf_op jit(solution)/shard_map/stack | solution.py:90
  912.8 8.5 reduce_sum.18
  943.9 5.4 collective-permute-start.36
  949.3 4.3 copy.1595
  953.9 8.2 reshape_reshape.64
  962.1 3.8 slice.1518
  967.4 4.8 copy.1539
  972.2 3.6 slice_select_fusion
  975.8 4.9 copy.1537
  987.2 3.7 pad_maximum_fusion.8
  990.9 8.8 copy.1540
  999.7 8.4 reduce_sum.19
  1011.7 5.4 collective-permute-start.38
  1017.2 11.8 %fusion.177 = (f32[4,27,1,4,1,4,1,4]{7,6,5,4,3,2,1,0:T(1,128)}, f32[4,27,1,4,1,4,1,4]{7,6,5,4,3,2,1,0:T(1,128)}, f32[4,27,1,4,1,4,1,4]{7,6,5,4,3,2,1,0:T(1,128)}...) fusion(f32[4,27,2,4,2,4,2,4]{7,6,5,4,3,2,1,0:T(2,128)} %reshape, ...), kind=kLoop, calls=%fused_computation.681 | loop fusion | bytes 442368 | tf_op jit(solution)/shard_map/slice | solution.py:148
  1039.4 3.5 copy.1738
  1047.5 7.2 copy.1612
  1054.6 6.7 reshape.1274
  (1147 shorter events, 706.7 us)
Async XLA Ops:
  0.6 13.1 %copy-start.72 = (f32[3,3,1,1,1]{1,0,4,3,2:T(4,128)S(1)}, f32[3,3,1,1,1]{1,0,4,3,2:T(4,128)}, u32[]{:S(2)}) copy-start(f32[3,3,1,1,1]{1,0,4,3,2:T(4,128)} %constant.750) | copy-start | bytes 112
  0.6 14.7 %copy-start.70 = (f32[3,3,1,1,1]{1,0,4,3,2:T(4,128)S(1)}, f32[3,3,1,1,1]{1,0,4,3,2:T(4,128)}, u32[]{:S(2)}) copy-start(f32[3,3,1,1,1]{1,0,4,3,2:T(4,128)} %constant.751) | copy-start | bytes 112
  0.7 14.0 %copy-start.148 = (f32[2,512]{1,0:T(2,128)S(1)}, f32[2,512]{1,0:T(2,128)}, u32[]{:S(2)}) copy-start(f32[2,512]{1,0:T(2,128)} %param.31) | copy-start | bytes 12292
  1.6 14.9 %copy-start.62 = (f32[1,54,512]{2,1,0:T(8,128)}, f32[1,54,512]{2,1,0:T(8,128)S(1)}, u32[]{:S(2)}) copy-start(f32[1,54,512]{2,1,0:T(8,128)S(1)} %reshape.1212) | copy-start | bytes 331780
  2.7 13.8 %copy-start.60 = (f32[1,108,512]{2,1,0:T(8,128)}, f32[1,108,512]{2,1,0:T(8,128)S(1)}, u32[]{:S(2)}) copy-start(f32[1,108,512]{2,1,0:T(8,128)S(1)} %reshape.1213) | copy-start | bytes 663556
  3.6 100.8 %collective-permute-start.1 = (f32[1,162,512]{2,1,0:T(8,128)}, f32[1,162,512]{2,1,0:T(8,128)}, u32[]{:S(2)}, u32[]{:S(2)}) collective-permute-start(f32[1,162,512]{2,1,0:T(8,128)} %pad_maximum_fusion.31), channel_id=1, source_target_pairs={{1,0},{2,1},{3,2},{4,3},{5,4},{6,5},{7,6},{8,7},{9,8},{10,9},{11,1... | collective-permute-start | bytes 995336 | tf_op jit(solution)/shard_map/ppermute | solution.py:22
  6.2 98.2 %collective-permute-start = (f32[1,162,512]{2,1,0:T(8,128)}, f32[1,162,512]{2,1,0:T(8,128)}, u32[]{:S(2)}, u32[]{:S(2)}) collective-permute-start(f32[1,162,512]{2,1,0:T(8,128)} %pad_maximum_fusion.31), channel_id=1, source_target_pairs={{0,1},{1,2},{2,3},{3,4},{4,5},{5,6},{6,7},{7,8},{8,9},{9,10},{10,1... | collective-permute-start | bytes 995336 | tf_op jit(solution)/shard_map/ppermute | solution.py:21
  17.6 14.0 %copy-start.107 = (s32[4,8]{1,0:T(4,128)S(1)}, s32[4,8]{1,0:T(4,128)}, u32[]{:S(2)}) copy-start(s32[4,8]{1,0:T(4,128)} %param.41) | copy-start | bytes 388
  18.1 29.8 %collective-permute-start.41 = (f32[1,36,64]{2,1,0:T(8,128)S(1)}, f32[1,36,64]{2,1,0:T(8,128)S(1)}, u32[]{:S(2)}, u32[]{:S(2)}) collective-permute-start(f32[1,36,64]{2,1,0:T(8,128)S(1)} %reshape.1265), channel_id=1, source_target_pairs={{1,0},{2,1},{3,2},{4,3},{5,4},{6,5},{7,6},{8,7},{9,8},{10,9},{11,1... | collective-permute-start | bytes 27656 | tf_op jit(solution)/shard_map/ppermute | solution.py:22
  20.0 27.9 %collective-permute-start.40 = (f32[1,36,64]{2,1,0:T(8,128)S(1)}, f32[1,36,64]{2,1,0:T(8,128)S(1)}, u32[]{:S(2)}, u32[]{:S(2)}) collective-permute-start(f32[1,36,64]{2,1,0:T(8,128)S(1)} %reshape.1265), channel_id=1, source_target_pairs={{0,1},{1,2},{2,3},{3,4},{4,5},{5,6},{6,7},{7,8},{8,9},{9,10},{10,1... | collective-permute-start | bytes 27656 | tf_op jit(solution)/shard_map/ppermute | solution.py:21
  50.5 8.0 collective-permute-start.43
  52.4 6.3 collective-permute-start.42
  61.0 12.3 %copy-start.87 = (f32[8,27,512]{2,0,1:T(8,128)S(1)}, f32[8,27,512]{2,0,1:T(8,128)}, u32[]{:S(2)}) copy-start(f32[8,27,512]{2,0,1:T(8,128)} %param.30) | copy-start | bytes 1327108
  62.0 13.6 %collective-permute-start.45 = (f32[1,36,64]{2,1,0:T(8,128)S(1)}, f32[1,36,64]{2,1,0:T(8,128)S(1)}, u32[]{:S(2)}, u32[]{:S(2)}) collective-permute-start(f32[1,36,64]{2,1,0:T(8,128)S(1)} %reshape.1269), channel_id=1, source_target_pairs={{1,0},{2,1},{3,2},{4,3},{5,4},{6,5},{7,6},{8,7},{9,8},{10,9},{11,1... | collective-permute-start | bytes 27656 | tf_op jit(solution)/shard_map/ppermute | solution.py:22
  63.9 11.7 %collective-permute-start.44 = (f32[1,36,64]{2,1,0:T(8,128)S(1)}, f32[1,36,64]{2,1,0:T(8,128)S(1)}, u32[]{:S(2)}, u32[]{:S(2)}) collective-permute-start(f32[1,36,64]{2,1,0:T(8,128)S(1)} %reshape.1269), channel_id=1, source_target_pairs={{0,1},{1,2},{2,3},{3,4},{4,5},{5,6},{6,7},{7,8},{8,9},{9,10},{10,1... | collective-permute-start | bytes 27656 | tf_op jit(solution)/shard_map/ppermute | solution.py:21
  91.4 12.0 %copy-start.64 = (f32[2,27,1,4,1,4,1,4]{7,6,5,4,3,2,0,1:T(1,128)S(1)}, f32[2,27,1,4,1,4,1,4]{7,6,5,4,3,2,0,1:T(1,128)}, u32[]{:S(2)}) copy-start(f32[2,27,1,4,1,4,1,4]{7,6,5,4,3,2,0,1:T(1,128)} %get-tuple-element.126) | copy-start | bytes 41476
  91.4 13.0 %copy-start.61 = (f32[1,108,512]{2,1,0:T(8,128)S(1)}, f32[1,108,512]{2,1,0:T(8,128)}, u32[]{:S(2)}) copy-start(f32[1,108,512]{2,1,0:T(8,128)} %copy-done.60) | copy-start | bytes 663556
  91.4 13.0 %copy-start.63 = (f32[1,54,512]{2,1,0:T(8,128)S(1)}, f32[1,54,512]{2,1,0:T(8,128)}, u32[]{:S(2)}) copy-start(f32[1,54,512]{2,1,0:T(8,128)} %copy-done.62) | copy-start | bytes 331780
  125.0 78.0 %collective-permute-start.3 = (f32[1,72,64]{2,1,0:T(8,128)}, f32[1,72,64]{2,1,0:T(8,128)}, u32[]{:S(2)}, u32[]{:S(2)}) collective-permute-start(f32[1,72,64]{2,1,0:T(8,128)} %reshape.1218), channel_id=1, source_target_pairs={{1,0},{2,1},{3,2},{4,3},{5,4},{6,5},{7,6},{8,7},{9,8},{10,9},{11,1... | collective-permute-start | bytes 55304 | tf_op jit(solution)/shard_map/ppermute | solution.py:22
  126.9 76.0 %collective-permute-start.2 = (f32[1,72,64]{2,1,0:T(8,128)}, f32[1,72,64]{2,1,0:T(8,128)}, u32[]{:S(2)}, u32[]{:S(2)}) collective-permute-start(f32[1,72,64]{2,1,0:T(8,128)} %reshape.1218), channel_id=1, source_target_pairs={{0,1},{1,2},{2,3},{3,4},{4,5},{5,6},{6,7},{7,8},{8,9},{9,10},{10,1... | collective-permute-start | bytes 55304 | tf_op jit(solution)/shard_map/ppermute | solution.py:21
  190.8 46.4 %collective-permute-start.15 = (f32[1,144,64]{2,1,0:T(8,128)}, f32[1,144,64]{2,1,0:T(8,128)}, u32[]{:S(2)}, u32[]{:S(2)}) collective-permute-start(f32[1,144,64]{2,1,0:T(8,128)} %reshape.1235), channel_id=1, source_target_pairs={{1,0},{2,1},{3,2},{4,3},{5,4},{6,5},{7,6},{8,7},{9,8},{10,9},{11,1... | collective-permute-start | bytes 110600 | tf_op jit(solution)/shard_map/ppermute | solution.py:22
  192.7 44.5 %collective-permute-start.14 = (f32[1,144,64]{2,1,0:T(8,128)}, f32[1,144,64]{2,1,0:T(8,128)}, u32[]{:S(2)}, u32[]{:S(2)}) collective-permute-start(f32[1,144,64]{2,1,0:T(8,128)} %reshape.1235), channel_id=1, source_target_pairs={{0,1},{1,2},{2,3},{3,4},{4,5},{5,6},{6,7},{7,8},{8,9},{9,10},{10,1... | collective-permute-start | bytes 110600 | tf_op jit(solution)/shard_map/ppermute | solution.py:21
  229.9 27.6 %collective-permute-start.5 = (f32[1,72,64]{2,1,0:T(8,128)}, f32[1,72,64]{2,1,0:T(8,128)}, u32[]{:S(2)}, u32[]{:S(2)}) collective-permute-start(f32[1,72,64]{2,1,0:T(8,128)} %reshape.1220), channel_id=1, source_target_pairs={{1,0},{2,1},{3,2},{4,3},{5,4},{6,5},{7,6},{8,7},{9,8},{10,9},{11,1... | collective-permute-start | bytes 55304 | tf_op jit(solution)/shard_map/ppermute | solution.py:22
  231.8 25.6 %collective-permute-start.4 = (f32[1,72,64]{2,1,0:T(8,128)}, f32[1,72,64]{2,1,0:T(8,128)}, u32[]{:S(2)}, u32[]{:S(2)}) collective-permute-start(f32[1,72,64]{2,1,0:T(8,128)} %reshape.1220), channel_id=1, source_target_pairs={{0,1},{1,2},{2,3},{3,4},{4,5},{5,6},{6,7},{7,8},{8,9},{9,10},{10,1... | collective-permute-start | bytes 55304 | tf_op jit(solution)/shard_map/ppermute | solution.py:21
  272.4 28.5 %collective-permute-start.7 = (f32[1,72,64]{2,1,0:T(8,128)}, f32[1,72,64]{2,1,0:T(8,128)}, u32[]{:S(2)}, u32[]{:S(2)}) collective-permute-start(f32[1,72,64]{2,1,0:T(8,128)} %reshape.1222), channel_id=1, source_target_pairs={{1,0},{2,1},{3,2},{4,3},{5,4},{6,5},{7,6},{8,7},{9,8},{10,9},{11,1... | collective-permute-start | bytes 55304 | tf_op jit(solution)/shard_map/ppermute | solution.py:22
  274.4 26.6 %collective-permute-start.6 = (f32[1,72,64]{2,1,0:T(8,128)}, f32[1,72,64]{2,1,0:T(8,128)}, u32[]{:S(2)}, u32[]{:S(2)}) collective-permute-start(f32[1,72,64]{2,1,0:T(8,128)} %reshape.1222), channel_id=1, source_target_pairs={{0,1},{1,2},{2,3},{3,4},{4,5},{5,6},{6,7},{7,8},{8,9},{9,10},{10,1... | collective-permute-start | bytes 55304 | tf_op jit(solution)/shard_map/ppermute | solution.py:21
  327.1 21.1 %collective-permute-start.9 = (f32[1,72,64]{2,1,0:T(8,128)S(1)}, f32[1,72,64]{2,1,0:T(8,128)S(1)}, u32[]{:S(2)}, u32[]{:S(2)}) collective-permute-start(f32[1,72,64]{2,1,0:T(8,128)S(1)} %reshape.1225), channel_id=1, source_target_pairs={{1,0},{2,1},{3,2},{4,3},{5,4},{6,5},{7,6},{8,7},{9,8},{10,9},{11,1... | collective-permute-start | bytes 55304 | tf_op jit(solution)/shard_map/ppermute | solution.py:22
  329.1 19.8 %collective-permute-start.8 = (f32[1,72,64]{2,1,0:T(8,128)S(1)}, f32[1,72,64]{2,1,0:T(8,128)}, u32[]{:S(2)}, u32[]{:S(2)}) collective-permute-start(f32[1,72,64]{2,1,0:T(8,128)S(1)} %reshape.1225), channel_id=1, source_target_pairs={{0,1},{1,2},{2,3},{3,4},{4,5},{5,6},{6,7},{7,8},{8,9},{9,10},{10,1... | collective-permute-start | bytes 55304 | tf_op jit(solution)/shard_map/ppermute | solution.py:21
  339.7 38.2 %collective-permute-start.17 = (f32[1,144,64]{2,1,0:T(8,128)}, f32[1,144,64]{2,1,0:T(8,128)}, u32[]{:S(2)}, u32[]{:S(2)}) collective-permute-start(f32[1,144,64]{2,1,0:T(8,128)} %reshape.1237), channel_id=1, source_target_pairs={{1,0},{2,1},{3,2},{4,3},{5,4},{6,5},{7,6},{8,7},{9,8},{10,9},{11,1... | collective-permute-start | bytes 110600 | tf_op jit(solution)/shard_map/ppermute | solution.py:22
  341.6 36.3 %collective-permute-start.16 = (f32[1,144,64]{2,1,0:T(8,128)}, f32[1,144,64]{2,1,0:T(8,128)}, u32[]{:S(2)}, u32[]{:S(2)}) collective-permute-start(f32[1,144,64]{2,1,0:T(8,128)} %reshape.1237), channel_id=1, source_target_pairs={{0,1},{1,2},{2,3},{3,4},{4,5},{5,6},{6,7},{7,8},{8,9},{9,10},{10,1... | collective-permute-start | bytes 110600 | tf_op jit(solution)/shard_map/ppermute | solution.py:21
  361.6 29.9 %copy-start.10 = (f32[8,3,1,3,8,8,8]{6,5,4,0,1,3,2:T(8,128)S(1)}, f32[8,3,1,3,8,8,8]{6,5,4,0,1,3,2:T(8,128)}, u32[]{:S(2)}) copy-start(f32[8,3,1,3,8,8,8]{6,5,4,0,1,3,2:T(8,128)} %copy-done.9) | copy-start | bytes 442372
  370.5 56.9 %collective-permute-start.11 = (f32[1,72,64]{2,1,0:T(8,128)}, f32[1,72,64]{2,1,0:T(8,128)}, u32[]{:S(2)}, u32[]{:S(2)}) collective-permute-start(f32[1,72,64]{2,1,0:T(8,128)} %reshape.1227), channel_id=1, source_target_pairs={{1,0},{2,1},{3,2},{4,3},{5,4},{6,5},{7,6},{8,7},{9,8},{10,9},{11,1... | collective-permute-start | bytes 55304 | tf_op jit(solution)/shard_map/ppermute | solution.py:22
  372.4 55.0 %collective-permute-start.10 = (f32[1,72,64]{2,1,0:T(8,128)}, f32[1,72,64]{2,1,0:T(8,128)}, u32[]{:S(2)}, u32[]{:S(2)}) collective-permute-start(f32[1,72,64]{2,1,0:T(8,128)} %reshape.1227), channel_id=1, source_target_pairs={{0,1},{1,2},{2,3},{3,4},{4,5},{5,6},{6,7},{7,8},{8,9},{9,10},{10,1... | collective-permute-start | bytes 55304 | tf_op jit(solution)/shard_map/ppermute | solution.py:21
  412.5 34.6 %collective-permute-start.19 = (f32[1,144,64]{2,1,0:T(8,128)}, f32[1,144,64]{2,1,0:T(8,128)}, u32[]{:S(2)}, u32[]{:S(2)}) collective-permute-start(f32[1,144,64]{2,1,0:T(8,128)} %reshape.1239), channel_id=1, source_target_pairs={{1,0},{2,1},{3,2},{4,3},{5,4},{6,5},{7,6},{8,7},{9,8},{10,9},{11,1... | collective-permute-start | bytes 110600 | tf_op jit(solution)/shard_map/ppermute | solution.py:22
  414.4 32.6 %collective-permute-start.18 = (f32[1,144,64]{2,1,0:T(8,128)}, f32[1,144,64]{2,1,0:T(8,128)}, u32[]{:S(2)}, u32[]{:S(2)}) collective-permute-start(f32[1,144,64]{2,1,0:T(8,128)} %reshape.1239), channel_id=1, source_target_pairs={{0,1},{1,2},{2,3},{3,4},{4,5},{5,6},{6,7},{7,8},{8,9},{9,10},{10,1... | collective-permute-start | bytes 110600 | tf_op jit(solution)/shard_map/ppermute | solution.py:21
  510.7 12.8 %collective-permute-start.21 = (f32[1,144,64]{2,1,0:T(8,128)S(1)}, f32[1,144,64]{2,1,0:T(8,128)S(1)}, u32[]{:S(2)}, u32[]{:S(2)}) collective-permute-start(f32[1,144,64]{2,1,0:T(8,128)S(1)} %reshape.1242), channel_id=1, source_target_pairs={{1,0},{2,1},{3,2},{4,3},{5,4},{6,5},{7,6},{8,7},{9,8},{10,9},{11,1... | collective-permute-start | bytes 110600 | tf_op jit(solution)/shard_map/ppermute | solution.py:22
  512.6 10.8 %collective-permute-start.20 = (f32[1,144,64]{2,1,0:T(8,128)S(1)}, f32[1,144,64]{2,1,0:T(8,128)S(1)}, u32[]{:S(2)}, u32[]{:S(2)}) collective-permute-start(f32[1,144,64]{2,1,0:T(8,128)S(1)} %reshape.1242), channel_id=1, source_target_pairs={{0,1},{1,2},{2,3},{3,4},{4,5},{5,6},{6,7},{7,8},{8,9},{9,10},{10,1... | collective-permute-start | bytes 110600 | tf_op jit(solution)/shard_map/ppermute | solution.py:21
  539.1 18.9 %collective-permute-start.23 = (f32[1,144,64]{2,1,0:T(8,128)}, f32[1,144,64]{2,1,0:T(8,128)}, u32[]{:S(2)}, u32[]{:S(2)}) collective-permute-start(f32[1,144,64]{2,1,0:T(8,128)} %reshape.1244), channel_id=1, source_target_pairs={{1,0},{2,1},{3,2},{4,3},{5,4},{6,5},{7,6},{8,7},{9,8},{10,9},{11,1... | collective-permute-start | bytes 110600 | tf_op jit(solution)/shard_map/ppermute | solution.py:22
  541.0 17.0 %collective-permute-start.22 = (f32[1,144,64]{2,1,0:T(8,128)}, f32[1,144,64]{2,1,0:T(8,128)}, u32[]{:S(2)}, u32[]{:S(2)}) collective-permute-start(f32[1,144,64]{2,1,0:T(8,128)} %reshape.1244), channel_id=1, source_target_pairs={{0,1},{1,2},{2,3},{3,4},{4,5},{5,6},{6,7},{7,8},{8,9},{9,10},{10,1... | collective-permute-start | bytes 110600 | tf_op jit(solution)/shard_map/ppermute | solution.py:21
  547.1 53.5 %collective-permute-start.13 = (f32[1,72,64]{2,1,0:T(8,128)}, f32[1,72,64]{2,1,0:T(8,128)}, u32[]{:S(2)}, u32[]{:S(2)}) collective-permute-start(f32[1,72,64]{2,1,0:T(8,128)} %reshape.1229), channel_id=1, source_target_pairs={{1,0},{2,1},{3,2},{4,3},{5,4},{6,5},{7,6},{8,7},{9,8},{10,9},{11,1... | collective-permute-start | bytes 55304 | tf_op jit(solution)/shard_map/ppermute | solution.py:22
  549.2 51.4 %collective-permute-start.12 = (f32[1,72,64]{2,1,0:T(8,128)}, f32[1,72,64]{2,1,0:T(8,128)}, u32[]{:S(2)}, u32[]{:S(2)}) collective-permute-start(f32[1,72,64]{2,1,0:T(8,128)} %reshape.1229), channel_id=1, source_target_pairs={{0,1},{1,2},{2,3},{3,4},{4,5},{5,6},{6,7},{7,8},{8,9},{9,10},{10,1... | collective-permute-start | bytes 55304 | tf_op jit(solution)/shard_map/ppermute | solution.py:21
  558.0 14.4 %copy-start.12 = (f32[8,3,3,8,8,8]{5,4,3,0,2,1:T(8,128)S(1)}, f32[8,3,3,8,8,8]{5,4,3,0,2,1:T(8,128)}, u32[]{:S(2)}) copy-start(f32[8,3,3,8,8,8]{5,4,3,0,2,1:T(8,128)} %copy-done.11) | copy-start | bytes 442372
  593.0 25.5 %collective-permute-start.25 = (f32[1,144,64]{2,1,0:T(8,128)}, f32[1,144,64]{2,1,0:T(8,128)}, u32[]{:S(2)}, u32[]{:S(2)}) collective-permute-start(f32[1,144,64]{2,1,0:T(8,128)} %reshape.1246), channel_id=1, source_target_pairs={{1,0},{2,1},{3,2},{4,3},{5,4},{6,5},{7,6},{8,7},{9,8},{10,9},{11,1... | collective-permute-start | bytes 110600 | tf_op jit(solution)/shard_map/ppermute | solution.py:22
  594.9 23.5 %collective-permute-start.24 = (f32[1,144,64]{2,1,0:T(8,128)}, f32[1,144,64]{2,1,0:T(8,128)}, u32[]{:S(2)}, u32[]{:S(2)}) collective-permute-start(f32[1,144,64]{2,1,0:T(8,128)} %reshape.1246), channel_id=1, source_target_pairs={{0,1},{1,2},{2,3},{3,4},{4,5},{5,6},{6,7},{7,8},{8,9},{9,10},{10,1... | collective-permute-start | bytes 110600 | tf_op jit(solution)/shard_map/ppermute | solution.py:21
  690.4 21.9 %collective-permute-start.27 = (f32[1,144,64]{2,1,0:T(8,128)}, f32[1,144,64]{2,1,0:T(8,128)}, u32[]{:S(2)}, u32[]{:S(2)}) collective-permute-start(f32[1,144,64]{2,1,0:T(8,128)} %reshape.1249), channel_id=1, source_target_pairs={{1,0},{2,1},{3,2},{4,3},{5,4},{6,5},{7,6},{8,7},{9,8},{10,9},{11,1... | collective-permute-start | bytes 110600 | tf_op jit(solution)/shard_map/ppermute | solution.py:22
  692.3 20.0 %collective-permute-start.26 = (f32[1,144,64]{2,1,0:T(8,128)}, f32[1,144,64]{2,1,0:T(8,128)}, u32[]{:S(2)}, u32[]{:S(2)}) collective-permute-start(f32[1,144,64]{2,1,0:T(8,128)} %reshape.1249), channel_id=1, source_target_pairs={{0,1},{1,2},{2,3},{3,4},{4,5},{5,6},{6,7},{7,8},{8,9},{9,10},{10,1... | collective-permute-start | bytes 110600 | tf_op jit(solution)/shard_map/ppermute | solution.py:21
  735.2 19.2 %copy-start.8 = (f32[4,3,3,8,8,8]{5,4,3,0,2,1:T(8,128)S(1)}, f32[4,3,3,8,8,8]{5,4,3,0,2,1:T(8,128)}, u32[]{:S(2)}) copy-start(f32[4,3,3,8,8,8]{5,4,3,0,2,1:T(8,128)} %get-tuple-element.129) | copy-start | bytes 221188
  735.2 19.2 %copy-start.57 = (f32[4,3,3,8,8,1]{5,4,3,0,2,1:T(8,128)S(1)}, f32[4,3,3,8,8,1]{5,4,3,0,2,1:T(8,128)}, u32[]{:S(2)}) copy-start(f32[4,3,3,8,8,1]{5,4,3,0,2,1:T(8,128)} %copy.1382) | copy-start | bytes 27652
  746.7 11.5 %collective-permute-start.29 = (f32[1,144,64]{2,1,0:T(8,128)}, f32[1,144,64]{2,1,0:T(8,128)S(1)}, u32[]{:S(2)}, u32[]{:S(2)}) collective-permute-start(f32[1,144,64]{2,1,0:T(8,128)} %reshape.1251), channel_id=1, source_target_pairs={{1,0},{2,1},{3,2},{4,3},{5,4},{6,5},{7,6},{8,7},{9,8},{10,9},{11,1... | collective-permute-start | bytes 110600 | tf_op jit(solution)/shard_map/ppermute | solution.py:22
  748.7 9.4 collective-permute-start.28
  758.1 13.4 %copy-start.18 = (f32[8,3,3,8,8,8]{5,4,3,0,1,2:T(8,128)S(1)}, f32[8,3,3,8,8,8]{5,4,3,0,1,2:T(8,128)}, u32[]{:S(2)}) copy-start(f32[8,3,3,8,8,8]{5,4,3,0,1,2:T(8,128)} %copy-done.17) | copy-start | bytes 442372
  792.1 15.5 %collective-permute-start.31 = (f32[1,144,64]{2,1,0:T(8,128)}, f32[1,144,64]{2,1,0:T(8,128)}, u32[]{:S(2)}, u32[]{:S(2)}) collective-permute-start(f32[1,144,64]{2,1,0:T(8,128)} %reshape.1253), channel_id=1, source_target_pairs={{1,0},{2,1},{3,2},{4,3},{5,4},{6,5},{7,6},{8,7},{9,8},{10,9},{11,1... | collective-permute-start | bytes 110600 | tf_op jit(solution)/shard_map/ppermute | solution.py:22
  794.0 13.6 %collective-permute-start.30 = (f32[1,144,64]{2,1,0:T(8,128)}, f32[1,144,64]{2,1,0:T(8,128)}, u32[]{:S(2)}, u32[]{:S(2)}) collective-permute-start(f32[1,144,64]{2,1,0:T(8,128)} %reshape.1253), channel_id=1, source_target_pairs={{0,1},{1,2},{2,3},{3,4},{4,5},{5,6},{6,7},{7,8},{8,9},{9,10},{10,1... | collective-permute-start | bytes 110600 | tf_op jit(solution)/shard_map/ppermute | solution.py:21
  853.1 18.6 %copy-start.55 = (f32[4,3,3,8,8,7]{5,4,3,0,2,1:T(8,128)S(1)}, f32[4,3,3,8,8,7]{5,4,3,0,2,1:T(8,128)}, u32[]{:S(2)}) copy-start(f32[4,3,3,8,8,7]{5,4,3,0,2,1:T(8,128)} %slice.1394) | copy-start | bytes 193540
  864.2 13.3 %collective-permute-start.33 = (f32[1,144,64]{2,1,0:T(8,128)}, f32[1,144,64]{2,1,0:T(8,128)S(1)}, u32[]{:S(2)}, u32[]{:S(2)}) collective-permute-start(f32[1,144,64]{2,1,0:T(8,128)} %reshape.1256), channel_id=1, source_target_pairs={{1,0},{2,1},{3,2},{4,3},{5,4},{6,5},{7,6},{8,7},{9,8},{10,9},{11,1... | collective-permute-start | bytes 110600 | tf_op jit(solution)/shard_map/ppermute | solution.py:22
  866.3 11.2 %collective-permute-start.32 = (f32[1,144,64]{2,1,0:T(8,128)}, f32[1,144,64]{2,1,0:T(8,128)S(1)}, u32[]{:S(2)}, u32[]{:S(2)}) collective-permute-start(f32[1,144,64]{2,1,0:T(8,128)} %reshape.1256), channel_id=1, source_target_pairs={{0,1},{1,2},{2,3},{3,4},{4,5},{5,6},{6,7},{7,8},{8,9},{9,10},{10,1... | collective-permute-start | bytes 110600 | tf_op jit(solution)/shard_map/ppermute | solution.py:21
  891.0 32.9 %collective-permute-start.35 = (f32[1,144,64]{2,1,0:T(8,128)}, f32[1,144,64]{2,1,0:T(8,128)}, u32[]{:S(2)}, u32[]{:S(2)}) collective-permute-start(f32[1,144,64]{2,1,0:T(8,128)} %reshape.1258), channel_id=1, source_target_pairs={{1,0},{2,1},{3,2},{4,3},{5,4},{6,5},{7,6},{8,7},{9,8},{10,9},{11,1... | collective-permute-start | bytes 110600 | tf_op jit(solution)/shard_map/ppermute | solution.py:22
  892.9 30.9 %collective-permute-start.34 = (f32[1,144,64]{2,1,0:T(8,128)}, f32[1,144,64]{2,1,0:T(8,128)}, u32[]{:S(2)}, u32[]{:S(2)}) collective-permute-start(f32[1,144,64]{2,1,0:T(8,128)} %reshape.1258), channel_id=1, source_target_pairs={{0,1},{1,2},{2,3},{3,4},{4,5},{5,6},{6,7},{7,8},{8,9},{9,10},{10,1... | collective-permute-start | bytes 110600 | tf_op jit(solution)/shard_map/ppermute | solution.py:21
  900.7 12.0 %copy-start.6 = (f32[4,3,3,3,8,8,8]{6,5,4,0,2,1,3:T(8,128)}, f32[4,3,3,3,8,8,8]{6,5,4,0,2,1,3:T(8,128)S(1)}, u32[]{:S(2)}) copy-start(f32[4,3,3,3,8,8,8]{6,5,4,0,2,1,3:T(8,128)S(1)} %pad_maximum_fusion.13) | copy-start | bytes 663556
  941.9 24.0 %collective-permute-start.37 = (f32[1,144,64]{2,1,0:T(8,128)S(1)}, f32[1,144,64]{2,1,0:T(8,128)S(1)}, u32[]{:S(2)}, u32[]{:S(2)}) collective-permute-start(f32[1,144,64]{2,1,0:T(8,128)S(1)} %reshape.1260), channel_id=1, source_target_pairs={{1,0},{2,1},{3,2},{4,3},{5,4},{6,5},{7,6},{8,7},{9,8},{10,9},{11,1... | collective-permute-start | bytes 110600 | tf_op jit(solution)/shard_map/ppermute | solution.py:22
  943.9 22.1 %collective-permute-start.36 = (f32[1,144,64]{2,1,0:T(8,128)S(1)}, f32[1,144,64]{2,1,0:T(8,128)S(1)}, u32[]{:S(2)}, u32[]{:S(2)}) collective-permute-start(f32[1,144,64]{2,1,0:T(8,128)S(1)} %reshape.1260), channel_id=1, source_target_pairs={{0,1},{1,2},{2,3},{3,4},{4,5},{5,6},{6,7},{7,8},{8,9},{9,10},{10,1... | collective-permute-start | bytes 110600 | tf_op jit(solution)/shard_map/ppermute | solution.py:21
  953.9 55.2 %copy-start.85 = (f32[1,108,64]{1,2,0:T(8,128)}, f32[1,108,64]{1,2,0:T(8,128)S(1)}, u32[]{:S(2)}) copy-start(f32[1,108,64]{1,2,0:T(8,128)S(1)} %mul.633) | copy-start | bytes 82948
  1009.8 51.6 %collective-permute-start.39 = (f32[1,324,64]{1,2,0:T(8,128)}, f32[1,324,64]{1,2,0:T(8,128)}, u32[]{:S(2)}, u32[]{:S(2)}) collective-permute-start(f32[1,324,64]{1,2,0:T(8,128)} %pad_maximum_fusion.59), channel_id=1, source_target_pairs={{1,0},{2,1},{3,2},{4,3},{5,4},{6,5},{7,6},{8,7},{9,8},{10,9},{11,1... | collective-permute-start | bytes 248840 | tf_op jit(solution)/shard_map/ppermute | solution.py:22
  1011.7 49.7 %collective-permute-start.38 = (f32[1,324,64]{1,2,0:T(8,128)}, f32[1,324,64]{1,2,0:T(8,128)}, u32[]{:S(2)}, u32[]{:S(2)}) collective-permute-start(f32[1,324,64]{1,2,0:T(8,128)} %pad_maximum_fusion.59), channel_id=1, source_target_pairs={{0,1},{1,2},{2,3},{3,4},{4,5},{5,6},{6,7},{7,8},{8,9},{9,10},{10,1... | collective-permute-start | bytes 248840 | tf_op jit(solution)/shard_map/ppermute | solution.py:21
  (153 other events, 598.6 us)
where the time goes:
time: 1090 us; the launch traced here: 1070 us
  local copies, waits for them, and re-layouts  634 us (58%)
  other arithmetic  218 us (20%)
  starting transfers between devices  172 us (16%)
  matrix products  42.7 us (4%)
    ppermute x23, starting transfers between devices, padded(): before = lax.ppermute(last, axis, up)  127 us
    unnamed x379, local copies, waits for them, and re-layouts  87.4 us
    gather x49, local copies, waits for them, and re-layouts, settle(): near[high_at, 1]  78.9 us
    gather x49, local copies, waits for them, and re-layouts, settle(): into_low = jnp.where((low_id >= 0)[:, None, None], near[low_at, 0], own_low)  78 us
    another operation x28, local copies, waits for them, and re-layouts, stream(): grid = jnp.stack([minus, rest, plus], axis=1 + axis)  73 us
    another operation x49, other arithmetic, stream(): grid = jnp.stack([minus, rest, plus], axis=1 + axis)  57.9 us
    another operation x70, local copies, waits for them, and re-layouts, face_block(): sent = jnp.stack([sent_high, sent_low], axis=1).reshape(1, count * 18, -1)  49.8 us
    ppermute x23, starting transfers between devices, padded(): after = lax.ppermute(first, axis, down)  45 us
  transfers between devices with their start and end apart: 46, of which 1 were waited for; matrix products, arithmetic and copies ran while one was open for 43% of the time, Pallas kernels for 0%

commit v1 on v0

--- a/solution.py
+++ b/solution.py
@@ -1,6 +1,10 @@
+import functools
+
 import jax
 import jax.numpy as jnp
 from jax import lax
+from jax.experimental import pallas as pl
+from jax.experimental.pallas import tpu as pltpu
 from jax.sharding import PartitionSpec as P
 
 C = 8
@@ -161,6 +165,308 @@
     count = field.shape[0]
     sent = jnp.stack([sent_high, sent_low], axis=1).reshape(1, count * 18, -1)
     return (sent, own_low, own_high)
+
+
+SLOTS = 16
+LANES = 128
+MESH = pl.DeviceIdType.MESH
+
+
+def forward(f, stride):
+    out = list(f)
+    for i in range(27):
+        if i // stride % 3 == 0:
+            lo, mid, hi = f[i], f[i + stride], f[i + 2 * stride]
+            both = lo + hi
+            out[i] = both + mid
+            out[i + stride] = hi - lo
+            out[i + 2 * stride] = both
+    return out
+
+
+def backward(m, stride):
+    out = list(m)
+    for i in range(27):
+        if i // stride % 3 == 0:
+            m0, m1, m2 = m[i], m[i + stride], m[i + 2 * stride]
+            out[i] = 0.5 * (m2 - m1)
+            out[i + stride] = m0 - m2
+            out[i + 2 * stride] = 0.5 * (m1 + m2)
+    return out
+
+
+def collide_row(f, keep, rate_ref):
+    for stride in (9, 3, 1):
+        f = forward(f, stride)
+    rho = f[0]
+    scale = keep / rho
+    mu = []
+    for k in (9, 3, 1):
+        v = f[k] * scale
+        mu.append((None, v, 1.0 / 3.0 + v * v))
+    for a in range(3):
+        ta = rho if a == 0 else rho * mu[0][a]
+        for b in range(3):
+            tb = ta if b == 0 else ta * mu[1][b]
+            for c in range(3):
+                t = tb if c == 0 else tb * mu[2][c]
+                i = 9 * a + 3 * b + c
+                f[i] = f[i] - rate_ref[i : i + 1, :] * (f[i] - t)
+    for stride in (9, 3, 1):
+        f = backward(f, stride)
+    return f
+
+
+def pick(v, idx):
+    return jnp.take_along_axis(v, idx, axis=1, mode="promise_in_bounds")
+
+
+def lbm_kernel(
+    n, n_fine, n_mid, f_ref, keep_ref, rate_ref, tab_ref, out_ref, P, Q, R, G, snap, S, RV, send_sem, recv_sem
+):
+    me = lax.axis_index("blk")
+    right, left = lax.rem(me + 1, n), lax.rem(me + n - 1, n)
+    barrier = pltpu.get_barrier_semaphore()
+
+    @pl.when(me > 0)
+    def _():
+        pl.semaphore_signal(barrier, inc=1, device_id=(left,), device_id_type=MESH)
+
+    @pl.when(me < n - 1)
+    def _():
+        pl.semaphore_signal(barrier, inc=1, device_id=(right,), device_id_type=MESH)
+
+    lane = lax.broadcasted_iota(jnp.int32, (8, LANES), 1)
+    lane64 = lax.broadcasted_iota(jnp.int32, (64, LANES), 1)
+    row64 = lax.broadcasted_iota(jnp.int32, (64, LANES), 0) % 8
+
+    def copies(slot):
+        out = []
+        for side, target in ((0, right), (1, left)):
+            out.append(
+                pltpu.make_async_remote_copy(
+                    src_ref=S.at[slot],
+                    dst_ref=RV.at[slot, side],
+                    send_sem=send_sem.at[slot, side],
+                    recv_sem=recv_sem.at[slot, side],
+                    device_id=(target,),
+                    device_id_type=MESH,
+                )
+            )
+        return out
+
+    def send(slot):
+        up, down = copies(slot)
+
+        @pl.when(me < n - 1)
+        def _():
+            up.start()
+
+        @pl.when(me > 0)
+        def _():
+            down.start()
+
+    def receive(slot):
+        up, down = copies(slot)
+
+        @pl.when(me < n - 1)
+        def _():
+            up.wait_send()
+            down.wait_recv()
+
+        @pl.when(me > 0)
+        def _():
+            down.wait_send()
+            up.wait_recv()
+
+    def own(slot, axis):
+        for d in range(2):
+            idx, dev = tab_ref[4 * axis + 2 * d], tab_ref[4 * axis + 2 * d + 1]
+            for j in range(9):
+                G[d, j] = jnp.where(dev == 0, pick(S[slot, d, j], idx), G[d, j])
+
+    def merge(slot, axis, d, j):
+        idx, dev = tab_ref[4 * axis + 2 * d], tab_ref[4 * axis + 2 * d + 1]
+        g = jnp.where(dev == -1, pick(RV[slot, 0, d, j], idx), G[d, j])
+        return jnp.where(dev == 1, pick(RV[slot, 1, d, j], idx), g)
+
+    def collide_at(x):
+        at = pl.ds(pl.multiple_of(8 * x, 8), 8)
+        f = collide_row([R[i, at, :] for i in range(27)], keep_ref[at, :], rate_ref)
+        to = pl.ds(pl.multiple_of(8 * x + 8, 8), 8)
+        for i in range(27):
+            P[i, to, :] = f[i]
+
+    def step_body(step, carry):
+        @pl.loop(0, 2)
+        def _(k):
+            collide_at(7 * k)
+
+        slot = 3 * step
+        for j in range(9):
+            S[slot, 0, j] = P[18 + j, 64:72, :]
+            S[slot, 1, j] = P[j, 8:16, :]
+
+        @pl.when(step == 0)
+        def _():
+            @pl.when((me == 0) | (me == n - 1))
+            def _():
+                pl.semaphore_wait(barrier, 1)
+
+            @pl.when((me > 0) & (me < n - 1))
+            def _():
+                pl.semaphore_wait(barrier, 2)
+
+        send(slot)
+
+        @pl.loop(1, 7)
+        def _(x):
+            collide_at(x)
+
+        for j in range(9):
+            G[0, j] = P[18 + j, 8:16, :]
+            G[1, j] = P[j, 64:72, :]
+        own(slot, 0)
+        receive(slot)
+        for j in range(9):
+            P[18 + j, 0:8, :] = merge(slot, 0, 0, j)
+            P[j, 72:80, :] = merge(slot, 0, 1, j)
+
+        slot = 3 * step + 1
+        for j in range(9):
+            a, c = j // 3, j % 3
+            plus, minus, base = 9 * a + 6 + c, 9 * a + c, 8 * (2 - a)
+            S[slot, 0, j] = P[plus, pl.ds(base + 7, 8, stride=8), :]
+            S[slot, 1, j] = P[minus, pl.ds(base, 8, stride=8), :]
+        send(slot)
+        for j in range(9):
+            a, c = j // 3, j % 3
+            plus, rest, minus, base = 9 * a + 6 + c, 9 * a + 3 + c, 9 * a + c, 8 * (2 - a)
+            G[0, j] = P[plus, pl.ds(base, 8, stride=8), :]
+            G[1, j] = P[minus, pl.ds(base + 7, 8, stride=8), :]
+            Q[rest] = P[rest, base : base + 64, :]
+            Q[plus] = pltpu.roll(P[plus, base : base + 64, :], 1, 0)
+            Q[minus] = pltpu.roll(P[minus, base : base + 64, :], 63, 0)
+        own(slot, 1)
+        receive(slot)
+        for j in range(9):
+            a, c = j // 3, j % 3
+            Q[9 * a + 6 + c, pl.ds(0, 8, stride=8), :] = merge(slot, 1, 0, j)
+            Q[9 * a + c, pl.ds(7, 8, stride=8), :] = merge(slot, 1, 1, j)
+
+        slot = 3 * step + 2
+        for j in range(9):
+            plus, minus = 3 * j + 2, 3 * j
+            hi = Q[plus, 56:64, :]
+            lo = Q[minus, 0:8, :]
+            for x in range(8):
+                if x < 7:
+                    v = pltpu.roll(Q[plus, 8 * x : 8 * x + 8, :], (16 * x + 16) % LANES, 1)
+                    hi = jnp.where(lane // 16 == x, v, hi)
+                if x > 0:
+                    v = pltpu.roll(Q[minus, 8 * x : 8 * x + 8, :], 16 * x, 1)
+                    lo = jnp.where(lane // 16 == x, v, lo)
+            S[slot, 0, j] = hi
+            S[slot, 1, j] = lo
+        send(slot)
+        for j in range(9):
+            plus, rest, minus = 3 * j + 2, 3 * j + 1, 3 * j
+            G[0, j] = jnp.zeros((8, LANES), jnp.float32)
+            G[1, j] = jnp.zeros((8, LANES), jnp.float32)
+            R[rest] = Q[rest]
+            v = Q[plus]
+            R[plus] = jnp.where(lane64 < 16, v, pltpu.roll(v, 16, 1))
+            v = Q[minus]
+            R[minus] = jnp.where(lane64 >= LANES - 16, v, pltpu.roll(v, LANES - 16, 1))
+        own(slot, 2)
+        receive(slot)
+        take_low = (lane < 16) & (tab_ref[9] != 2)
+        take_high = (lane >= LANES - 16) & (tab_ref[11] != 2)
+        for j in range(9):
+            low = merge(slot, 2, 0, j)
+            high = merge(slot, 2, 1, j)
+            for x in range(8):
+                at = slice(8 * x, 8 * x + 8)
+                v = low if x == 0 else pltpu.roll(low, (LANES - 16 * x) % LANES, 1)
+                R[3 * j + 2, at, :] = jnp.where(take_low, v, R[3 * j + 2, at, :])
+                v = high if x == 7 else pltpu.roll(high, (LANES - 16 - 16 * x) % LANES, 1)
+                R[3 * j, at, :] = jnp.where(take_high, v, R[3 * j, at, :])
+
+        @pl.when(step == 0)
+        def _():
+            snap[...] = R[...]
+
+        @pl.when(step == 1)
+        def _():
+            for i in range(27):
+                snap[i] = jnp.where(lane64 % SLOTS < n_fine + n_mid, R[i], snap[i])
+
+        return carry
+
+    R[...] = f_ref[...]
+    lax.fori_loop(0, 4, step_body, 0)
+    for i in range(27):
+        out_ref[i] = jnp.where(lane64 % SLOTS < n_fine, R[i], snap[i])
+
+
+def to_lanes(arrays):
+    k = arrays[0].shape[1]
+    pad = SLOTS - sum(a.shape[0] for a in arrays)
+    whole = jnp.concatenate(arrays + [jnp.ones((pad, k, 512), jnp.float32)], axis=0)
+    return whole.reshape(SLOTS, k * 64, 8).transpose(1, 2, 0).reshape(k, 64, LANES)
+
+
+def face_tables(tables, place):
+    ids, devs = [], []
+    base = 0
+    for table in tables:
+        count = table.shape[0]
+        group = table // count
+        ids.append(table - group * count + base)
+        devs.append(jnp.where(table < 0, 2, group - place))
+        base += count
+    pad = ((0, SLOTS - base), (0, 0))
+    ids = jnp.pad(jnp.concatenate(ids), pad).T
+    devs = jnp.pad(jnp.concatenate(devs), pad, constant_values=2).T
+    ids = jnp.clip(ids, 0, SLOTS - 1)
+    ids = ids[:, None, :] + SLOTS * jnp.arange(8, dtype=jnp.int32)[None, :, None]
+    devs = jnp.broadcast_to(devs[:, None, :], (6, 8, SLOTS))
+    both = jnp.stack([ids, devs], axis=1).reshape(12, 1, LANES)
+    return jnp.broadcast_to(both, (12, 8, LANES))
+
+
+def advance_all(fields, solids, rates, tables, place):
+    n = lax.axis_size("blk")
+    counts = [f.shape[0] for f in fields]
+    f_all = to_lanes(fields)
+    keep = 1.0 - to_lanes([s[:, None, :] for s in solids])[0]
+    level = [2] * counts[0] + [1] * counts[1] + [0] * (SLOTS - counts[0] - counts[1])
+    rate = jnp.stack([rates[k] for k in level], axis=1)
+    rate = jnp.tile(rate, (1, 8))
+    vmem = pl.BlockSpec(memory_space=pltpu.VMEM)
+    out = pl.pallas_call(
+        functools.partial(lbm_kernel, n, counts[0], counts[1]),
+        out_shape=jax.ShapeDtypeStruct((27, 64, LANES), jnp.float32),
+        in_specs=[vmem] * 4,
+        out_specs=vmem,
+        scratch_shapes=[
+            pltpu.VMEM((27, 80, LANES), jnp.float32),
+            pltpu.VMEM((27, 64, LANES), jnp.float32),
+            pltpu.VMEM((27, 64, LANES), jnp.float32),
+            pltpu.VMEM((2, 9, 8, LANES), jnp.float32),
+            pltpu.VMEM((27, 64, LANES), jnp.float32),
+            pltpu.VMEM((12, 2, 9, 8, LANES), jnp.float32),
+            pltpu.VMEM((12, 2, 2, 9, 8, LANES), jnp.float32),
+            pltpu.SemaphoreType.DMA((12, 2)),
+            pltpu.SemaphoreType.DMA((12, 2)),
+        ],
+        compiler_params=pltpu.CompilerParams(
+            collective_id=0, has_side_effects=True, vmem_limit_bytes=32 * 1024 * 1024
+        ),
+    )(f_all, keep, rate, face_tables(tables, place))
+    back = out.reshape(27 * 64, 8, SLOTS).transpose(2, 0, 1).reshape(SLOTS, 27, 512)
+    fine, mid = counts[0], counts[0] + counts[1]
+    return back[:fine], back[fine:mid], back[mid : mid + counts[2]]
 
 
 def local(
@@ -194,30 +500,11 @@
     pieces_fine = lookup(octant_table(mid_near, edge), explode_fine, (place - 1) * n_mid)
     mid_start = explode(f_mid, pieces_mid, explode_mid[:, 0], edge)
     fine_start = explode(f_fine, pieces_fine, explode_fine[:, 0], edge)
-    fields = [f_coarse, mid_start, fine_start]
-    solids = [solid_coarse, solid_mid, solid_fine]
-    neighbours = [faces_coarse, faces_mid, faces_fine]
-    substeps = [1, 2, 4]
-    for level in range(3):
-        field = fields[level]
-        count = field.shape[0]
-        for step in range(substeps[level]):
-            field = collide(field, solids[level], rates[level])
-            for axis in range(3):
-                sent, own_low, own_high = face_block(field, axis, edge)
-                near = padded(sent, (("blk", 0),), 1).reshape(3 * count, 2, 9, -1)
-                field = settle(
-                    field,
-                    axis,
-                    edge,
-                    near,
-                    neighbours[level],
-                    (place - 1) * count,
-                    own_low,
-                    own_high,
-                )
-        fields[level] = field
-    coarse, middle, fine_out = fields
+    solids = [solid_fine, solid_mid, solid_coarse]
+    tables = [faces_fine, faces_mid, faces_coarse]
+    fine_out, middle, coarse = advance_all(
+        [fine_start, mid_start, f_coarse], solids, rates, tables, place
+    )
     sent = jnp.concatenate(
         [
             restrict(middle, edge).reshape(1, n_mid * 27, -1),

time: 1090 us -> 265 us (0.24); the launches traced: 1070 us -> 261 us
  local copies, waits for them, and re-layouts: 634 us -> 141 us
  other arithmetic: 218 us -> 39.1 us
  starting transfers between devices: 172 us -> 14.7 us
  Pallas kernels: 0 us -> 63.9 us
  matrix products: 42.7 us -> 0 us
    another operation x122 -> x6, local copies, waits for them, and re-layouts: 164 us -> 0.26 us  [the longest x3 0.15 us: advance_all(): rate = jnp.stack([rates[k] for k in level], axis=1)]
    gather x98 -> x0, local copies, waits for them, and re-layouts: 157 us -> none  [the longest x49 78.9 us: settle(): near[high_at, 1]]
    ppermute x23 -> x2, starting transfers between devices: 127 us -> 10.2 us  [padded(): before = lax.ppermute(last, axis, up)]
    slice x98 -> x7, local copies, waits for them, and re-layouts: 137 us -> 21.1 us  [advance_all(): return (back[:fine], back[fine:mid], back[mid:mid + counts[2]])]
    another operation x84 -> x1, other arithmetic: 68.9 us -> 0.01 us  [face_tables(): both = jnp.stack([ids, devs], axis=1).reshape(12, 1, LANES)]
    pallas_call x0 -> x1, Pallas kernels: none -> 63.9 us  [advance_all(): pl.pallas_call(functools.partial(lbm_kernel, n, counts[0], counts[1]), ou...]
    select_n x41 -> x0, other arithmetic: 61.8 us -> none  [the longest x20 34.6 us: settle(): jnp.where((high_id >= 0)[:, None, None], near[high_at, 1], own_high)]
    unnamed x379 -> x154, local copies, waits for them, and re-layouts: 87.4 us -> 41.3 us
  transfers between devices with their start and end apart: 46 -> 4, of which waited for: 1 -> 0; matrix products, arithmetic and copies ran while one was open for 43% -> 36% of each run, Pallas kernels for 0% -> 0%
where the time goes in v1:
time: 265 us; the launch traced here: 261 us
  local copies, waits for them, and re-layouts  141 us (53%)
  Pallas kernels  63.9 us (24%)
  other arithmetic  39.1 us (15%)
  starting transfers between devices  14.7 us (6%)
    pallas_call x1, Pallas kernels, advance_all(): pl.pallas_call(functools.partial(lbm_kernel, n, counts[0], counts[1]), ou...  63.9 us
    unnamed x154, local copies, waits for them, and re-layouts  41.3 us
    slice x7, local copies, waits for them, and re-layouts, advance_all(): return (back[:fine], back[fine:mid], back[mid:mid + counts[2]])  21.1 us
    reshape x2, local copies, waits for them, and re-layouts, assemble(): grid = parent.reshape(count, 27, 2, half, 2, half, 2, half)  18.9 us
    reduce_sum x2, other arithmetic, restrict(): return (jnp.sum(grid, axis=(3, 5, 7)) * 0.125).reshape(count, 27, half ** 3)  16.7 us
    slice x2, local copies, waits for them, and re-layouts, assemble(): old = grid[:, :, octant // 4, :, octant // 2 % 2, :, octant % 2, :]  15.4 us
    ppermute x2, starting transfers between devices, padded(): before = lax.ppermute(last, axis, up)  10.2 us
    concatenate x8, local copies, waits for them, and re-layouts, to_lanes(): jnp.concatenate(arrays + [jnp.ones((pad, k, 512), jnp.float32)], axis=0)  9.27 us
  transfers between devices with their start and end apart: 4, of which 0 were waited for; matrix products, arithmetic and copies ran while one was open for 36% of the time, Pallas kernels for 0%

profile of v1, /device:TPU:23, one launch (start us, length us, event | category | flops | bytes accessed | tf_op | source)
XLA Modules:
  0.0 261.2 jit_solution(1586708374638787072)
XLA Ops:
  0.7 1.1 copy.332
  1.8 0.9 copy.331
  2.8 2.6 collective-permute-start.1
  5.4 4.8 %collective-permute-start = (f32[1,162,512]{2,1,0:T(8,128)S(1)}, f32[1,162,512]{2,1,0:T(8,128)S(1)}, u32[]{:S(2)}, u32[]{:S(2)}) collective-permute-start(f32[1,162,512]{2,1,0:T(8,128)S(1)} %pad_maximum_fusion.4), channel_id=1, source_target_pairs={{0,1},{1,2},{2,3},{3,4},{4,5},{5,6},{6,7},{7,8},{8,9},{9,10},{10,1... | collective-permute-start | bytes 995336 | tf_op jit(solution)/shard_map/ppermute | solution.py:25
  10.2 1.9 copy.346
  12.1 2.3 copy.345
  15.1 0.8 fusion.14
  16.5 1.9 compare_reduce_fusion.8
  18.4 0.8 fusion.19
  20.4 2.1 copy.337
  24.9 0.8 fusion.6
  25.8 0.8 broadcast_and_fusion
  26.6 0.8 broadcast_and_fusion.1
  28.6 0.8 reshape_reshape.9
  29.4 1.6 copy.340
  31.0 2.0 copy.342
  33.7 0.8 copy.343
  35.1 2.8 %reshape_reshape.8 = f32[12,27,2,4,2,4,2,4]{1,0,7,6,5,4,3,2:T(8,128)} reshape(f32[3,108,512]{1,0,2:T(4,128)S(1)} %copy.333) | data formatting | bytes 1327104 | tf_op jit(solution)/shard_map/reshape;reshape | solution.py:112
  37.8 3.4 %copy.334 = f32[12,2,2,2,27,4,4,4]{4,7,6,5,3,2,1,0:T(4,128)S(1)} copy(f32[12,2,2,2,27,4,4,4]{4,0,7,3,6,2,5,1:T(8,128)} %bitcast.133) | data formatting | bytes 1327104 | tf_op jit(solution)/shard_map/transpose | solution.py:112
  41.3 2.2 copy.335
  43.5 2.2 gather_fusion
  46.3 4.9 %copy_select_fusion = f32[4,27,512]{1,0,2:T(4,128)S(1)} fusion(f32[4,27,512]{1,0,2:T(4,128)} %copy.345, f32[4,27,512]{1,2,0:T(8,128)S(1)} %bitcast.137, pred[4,512]{0,1:T(8,128)(4,1)S(1)} %copy-done.29), kind=kLoop, calls=%fused_computation.7 | loop fusion | flops 55296 | bytes 665600 | tf_op jit(solution)/shard_map/jit(_where)/select_n | solution.py:136
  51.9 2.9 %maximum_maximum_fusion = f32[16,27,512]{1,0,2:T(8,128)} fusion(f32[2,27,512]{1,0,2:T(2,128)S(1)} %copy-done.6, f32[4,27,512]{1,0,2:T(4,128)S(1)} %copy_select_fusion, f32[8,27,512]{1,0,2:T(8,128)S(1)} %bitcast_select_fusion, f32[16]{0:T(128)S(1)} %copy-done.44), kind=kLoop, calls=%fused_computation.4 | loop fusion | flops 663552 | bytes 1658944 | tf_op jit(solution)/shard_map/concatenate | solution.py:415
  54.8 8.6 %copy.347 = f32[16,27,512]{0,2,1:T(8,128)} copy(f32[16,27,512]{1,0,2:T(8,128)} %maximum_maximum_fusion) | data formatting | bytes 1769472 | tf_op jit(solution)/shard_map/concatenate | solution.py:415
  63.4 4.5 %reshape.699.f_ref = f32[27,64,128]{2,1,0:T(8,128)S(1)} reshape(f32[1728,8,16]{2,1,0:T(8,128)} %bitcast.132) | data formatting | bytes 1769472 | tf_op jit(solution)/shard_map/reshape | solution.py:416
  67.9 63.9 %shard_map.157 = f32[27,64,128]{2,1,0:T(8,128)S(1)} custom-call(f32[27,64,128]{2,1,0:T(8,128)S(1)} %reshape.699.f_ref, f32[64,128]{1,0:T(8,128)S(1)} %copy.357.keep_ref, f32[27,128]{1,0:T(8,128)S(1)} %tile.10.rate_ref, s32[12,8,128]{2,1,0:T(8,128)S(1)} %broadcast_in_dim.186.tab_ref), custom_call_target="tpu_custom_call" | custom-call | tf_op jit(solution)/shard_map/pallas_call | solution.py:447
  131.8 2.8 %copy.358 = f32[27,64,128]{1,0,2:T(8,128)} copy(f32[27,64,128]{2,1,0:T(8,128)S(1)} %shard_map.157) | data formatting | bytes 1769472 | tf_op jit(solution)/shard_map/pallas_call | solution.py:447
  134.6 2.0 reshape.654
  136.7 4.4 %copy.362 = f32[8,1728,8]{0,2,1:T(8,128)} copy(f32[8,1728,8]{1,0,2:T(8,128)S(1)} %slice.279) | data formatting | bytes 884736 | tf_op jit(solution)/shard_map/slice | solution.py:469
  141.1 8.4 %reduce_sum.19 = f32[8,27,4,4,4]{0,4,3,2,1:T(4,128)S(1)} reduce(f32[8,27,4,2,4,2,4,2]{0,7,6,5,4,3,2,1:T(2,128)} %bitcast.131, f32[]{:T(128)} %constant.47.clone.1), dimensions={3,5,7}, to_apply=%region_1.2 | reduce | flops 96768 | bytes 497668 | tf_op jit(solution)/shard_map/reduce_sum | solution.py:143
  149.5 0.8 copy.363
  150.5 4.5 %copy.359 = f32[4,1728,8]{0,2,1:T(8,128)} copy(f32[4,1728,8]{1,0,2:T(4,128)S(1)} %slice.278) | data formatting | bytes 442368 | tf_op jit(solution)/shard_map/slice | solution.py:469
  154.9 8.4 %reduce_sum.18 = f32[4,27,4,4,4]{0,4,3,2,1:T(4,128)S(1)} reduce(f32[4,27,4,2,4,2,4,2]{0,7,6,5,4,3,2,1:T(2,128)} %bitcast.130, f32[]{:T(128)} %constant.47.clone.1), dimensions={3,5,7}, to_apply=%region_0.1 | reduce | flops 48384 | bytes 248836 | tf_op jit(solution)/shard_map/reduce_sum | solution.py:143
  163.3 0.9 copy.360
  164.5 0.7 pad_maximum_fusion.9
  165.2 1.9 collective-permute-start.3
  167.1 5.4 %collective-permute-start.2 = (f32[1,324,64]{1,2,0:T(8,128)}, f32[1,324,64]{1,2,0:T(8,128)}, u32[]{:S(2)}, u32[]{:S(2)}) collective-permute-start(f32[1,324,64]{1,2,0:T(8,128)} %pad_maximum_fusion.9), channel_id=1, source_target_pairs={{0,1},{1,2},{2,3},{3,4},{4,5},{5,6},{6,7},{7,8},{8,9},{9,10},{10,1... | collective-permute-start | bytes 248840 | tf_op jit(solution)/shard_map/ppermute | solution.py:25
  173.3 13.1 %reshape.701 = f32[4,27,2,4,2,4,2,4]{5,4,3,2,1,0,7,6:T(2,128)} reshape(f32[4,1728,8]{1,0,2:T(4,128)S(1)} %slice.278) | data formatting | bytes 442368 | tf_op jit(solution)/shard_map/reshape | solution.py:149
  186.3 5.9 %reshape.700 = f32[2,27,2,4,2,4,2,4]{5,4,3,2,1,0,7,6:T(2,128)S(1)} reshape(f32[2,1728,8]{1,0,2:T(2,128)} %slice.281) | data formatting | bytes 221184 | tf_op jit(solution)/shard_map/reshape | solution.py:149
  192.2 11.6 %fusion.15 = (f32[4,27,1,4,1,4,1,4]{5,4,3,2,1,0,7,6:T(1,128)}, f32[4,27,1,4,1,4,1,4]{5,4,3,2,1,0,7,6:T(1,128)}, f32[4,27,1,4,1,4,1,4]{5,4,3,2,1,0,7,6:T(1,128)},...) fusion(f32[4,27,2,4,2,4,2,4]{5,4,3,2,1,0,7,6:T(2,128)} %reshape.701), kind=kLoop, calls=%fused_computation.126 | loop fusion | bytes 442368 | tf_op jit(solution)/shard_map/slice | solution.py:152
  203.8 3.9 %fusion.16 = (f32[2,27,1,4,1,4,1,4]{5,4,3,2,1,0,7,6:T(1,128)}, f32[2,27,1,4,1,4,1,4]{5,4,3,2,1,0,7,6:T(1,128)}, f32[2,27,1,4,1,4,1,4]{5,4,3,2,1,0,7,6:T(1,128)},...) fusion(f32[2,27,2,4,2,4,2,4]{5,4,3,2,1,0,7,6:T(2,128)S(1)} %res, ...), kind=kLoop, calls=%fused_computation.127 | loop fusion | bytes 221184 | tf_op jit(solution)/shard_map/slice | solution.py:152
  207.7 5.3 %copy.404 = f32[8,1728,8]{2,1,0:T(8,128)} copy(f32[8,1728,8]{1,0,2:T(8,128)} %copy-done.1) | data formatting | bytes 884736 | tf_op jit(solution)/shard_map/slice | solution.py:469
  213.0 1.0 copy.422
  214.0 1.0 copy.421
  215.1 1.0 copy.420
  216.1 1.0 copy.419
  217.1 1.1 copy.418
  218.2 1.2 copy.417
  219.4 2.0 copy.416
  221.4 1.9 copy.415
  223.3 3.5 %copy.430 = f32[4,27,1,4,1,4,1,4]{1,7,5,3,0,6,4,2:T(4,128)} copy(f32[4,27,1,4,1,4,1,4]{5,4,3,2,1,0,7,6:T(1,128)} %get-tuple-element.41) | data formatting | bytes 55296
  226.8 3.5 %copy.429 = f32[4,27,1,4,1,4,1,4]{1,7,5,3,0,6,4,2:T(4,128)} copy(f32[4,27,1,4,1,4,1,4]{5,4,3,2,1,0,7,6:T(1,128)} %get-tuple-element.35) | data formatting | bytes 55296
  230.3 3.5 %copy.428 = f32[4,27,1,4,1,4,1,4]{1,7,5,3,0,6,4,2:T(4,128)} copy(f32[4,27,1,4,1,4,1,4]{5,4,3,2,1,0,7,6:T(1,128)} %get-tuple-element.36) | data formatting | bytes 55296
  233.9 3.5 %copy.427 = f32[4,27,1,4,1,4,1,4]{1,7,5,3,0,6,4,2:T(4,128)} copy(f32[4,27,1,4,1,4,1,4]{5,4,3,2,1,0,7,6:T(1,128)} %get-tuple-element.37) | data formatting | bytes 55296
  237.4 1.9 copy.426
  239.2 0.9 copy.425
  240.1 0.9 copy.424
  241.0 0.9 copy.423
  241.9 6.1 %slice.268 = f32[8,27,512]{2,1,0:T(8,128)S(1)} reshape(f32[8,1728,8]{2,1,0:T(8,128)} %copy.404) | data formatting | bytes 884736 | tf_op jit(solution)/shard_map/slice | solution.py:469
  248.2 1.0 copy.407
  249.2 0.9 pad_maximum_fusion.8
  253.5 0.8 copy.405
  254.3 1.0 pad_maximum_fusion.5
  260.0 1.0 copy.406
  (257 shorter events, 17.5 us)
Async XLA Ops:
  0.6 19.8 %copy-start.27 = (f32[8,27,512]{2,0,1:T(8,128)S(1)}, f32[8,27,512]{2,0,1:T(8,128)}, u32[]{:S(2)}) copy-start(f32[8,27,512]{2,0,1:T(8,128)} %param.16) | copy-start | bytes 1327108
  0.6 22.5 %copy-start.41 = (f32[2,512]{1,0:T(2,128)S(1)}, f32[2,512]{1,0:T(2,128)}, u32[]{:S(2)}) copy-start(f32[2,512]{1,0:T(2,128)} %param.17) | copy-start | bytes 12292
  0.7 22.6 %copy-start.40 = (f32[4,512]{1,0:T(4,128)S(1)}, f32[4,512]{1,0:T(4,128)}, u32[]{:S(2)}) copy-start(f32[4,512]{1,0:T(4,128)} %param.18) | copy-start | bytes 24580
  0.7 22.8 %copy-start.39 = (f32[8,512]{1,0:T(8,128)S(1)}, f32[8,512]{1,0:T(8,128)}, u32[]{:S(2)}) copy-start(f32[8,512]{1,0:T(8,128)} %param.19) | copy-start | bytes 49156
  0.7 23.4 %copy-start.62 = (f32[3,27]{1,0:T(4,128)S(1)}, f32[3,27]{1,0:T(4,128)}, u32[]{:S(2)}) copy-start(f32[3,27]{1,0:T(4,128)} %param.20) | copy-start | bytes 976
  0.7 23.7 %copy-start.63 = (s32[2,6]{1,0:T(2,128)S(1)}, s32[2,6]{1,0:T(2,128)}, u32[]{:S(2)}) copy-start(s32[2,6]{1,0:T(2,128)} %param.21) | copy-start | bytes 148
  0.7 23.7 %copy-start.61 = (s32[4,6]{1,0:T(4,128)S(1)}, s32[4,6]{1,0:T(4,128)}, u32[]{:S(2)}) copy-start(s32[4,6]{1,0:T(4,128)} %param.22) | copy-start | bytes 292
  0.7 23.7 %copy-start.42 = (s32[8,6]{1,0:T(8,128)S(1)}, s32[8,6]{1,0:T(8,128)}, u32[]{:S(2)}) copy-start(s32[8,6]{1,0:T(8,128)} %param.23) | copy-start | bytes 580
  1.8 23.1 %copy-start.38 = (s32[4,8]{1,0:T(4,128)S(1)}, s32[4,8]{1,0:T(4,128)}, u32[]{:S(2)}) copy-start(s32[4,8]{1,0:T(4,128)} %param.27) | copy-start | bytes 388
  2.8 24.6 %collective-permute-start.1 = (f32[1,162,512]{2,1,0:T(8,128)S(1)}, f32[1,162,512]{2,1,0:T(8,128)S(1)}, u32[]{:S(2)}, u32[]{:S(2)}) collective-permute-start(f32[1,162,512]{2,1,0:T(8,128)S(1)} %pad_maximum_fusion.4), channel_id=1, source_target_pairs={{1,0},{2,1},{3,2},{4,3},{5,4},{6,5},{7,6},{8,7},{9,8},{10,9},{11,1... | collective-permute-start | bytes 995336 | tf_op jit(solution)/shard_map/ppermute | solution.py:26
  5.4 22.0 %collective-permute-start = (f32[1,162,512]{2,1,0:T(8,128)S(1)}, f32[1,162,512]{2,1,0:T(8,128)S(1)}, u32[]{:S(2)}, u32[]{:S(2)}) collective-permute-start(f32[1,162,512]{2,1,0:T(8,128)S(1)} %pad_maximum_fusion.4), channel_id=1, source_target_pairs={{0,1},{1,2},{2,3},{3,4},{4,5},{5,6},{6,7},{7,8},{8,9},{9,10},{10,1... | collective-permute-start | bytes 995336 | tf_op jit(solution)/shard_map/ppermute | solution.py:25
  23.9 3.5 %copy-start.43 = (f32[16]{0:T(128)}, f32[16]{0:T(128)S(1)}, u32[]{:S(2)}) copy-start(f32[16]{0:T(128)S(1)} %pad.58.clone) | copy-start | bytes 196
  29.4 5.0 %copy-start.14 = (f32[1,162,512]{2,1,0:T(8,128)S(1)}, f32[1,162,512]{2,1,0:T(8,128)}, u32[]{:S(2)}) copy-start(f32[1,162,512]{2,1,0:T(8,128)} %copy-done.13) | copy-start | bytes 995332
  29.4 5.0 %copy-start.16 = (f32[1,162,512]{2,1,0:T(8,128)S(1)}, f32[1,162,512]{2,1,0:T(8,128)}, u32[]{:S(2)}) copy-start(f32[1,162,512]{2,1,0:T(8,128)} %copy-done.15) | copy-start | bytes 995332
  41.2 4.7 %copy-start.19 = (f32[4,27,64]{1,2,0:T(8,128)S(1)}, f32[4,27,64]{1,2,0:T(8,128)}, u32[]{:S(2)}) copy-start(f32[4,27,64]{1,2,0:T(8,128)} %copy.343) | copy-start | bytes 82948
  41.3 5.0 %copy-start.29 = (pred[4,512]{0,1:T(8,128)(4,1)S(1)}, pred[4,512]{0,1:T(8,128)(4,1)}, u32[]{:S(2)}) copy-start(pred[4,512]{0,1:T(8,128)(4,1)} %broadcast_and_fusion) | copy-start | bytes 6148
  41.3 9.9 %copy-start.28 = (pred[8,512]{0,1:T(8,128)(4,1)S(1)}, pred[8,512]{0,1:T(8,128)(4,1)}, u32[]{:S(2)}) copy-start(pred[8,512]{0,1:T(8,128)(4,1)} %broadcast_and_fusion.1) | copy-start | bytes 12292
  43.5 7.7 %copy-start = (f32[8,27,512]{1,0,2:T(8,128)S(1)}, f32[8,27,512]{1,0,2:T(8,128)}, u32[]{:S(2)}) copy-start(f32[8,27,512]{1,0,2:T(8,128)} %copy.337) | copy-start | bytes 1327108
  45.9 6.0 %copy-start.6 = (f32[2,27,512]{1,0,2:T(2,128)S(1)}, f32[2,27,512]{1,0,2:T(2,128)}, u32[]{:S(2)}) copy-start(f32[2,27,512]{1,0,2:T(2,128)} %copy.346) | copy-start | bytes 331780
  45.9 6.0 %copy-start.44 = (f32[16]{0:T(128)S(1)}, f32[16]{0:T(128)}, u32[]{:S(2)}) copy-start(f32[16]{0:T(128)} %copy-done.43) | copy-start | bytes 196
  136.7 12.8 %copy-start.1 = (f32[8,1728,8]{1,0,2:T(8,128)}, f32[8,1728,8]{1,0,2:T(8,128)S(1)}, u32[]{:S(2)}) copy-start(f32[8,1728,8]{1,0,2:T(8,128)S(1)} %slice.279) | copy-start | bytes 1327108
  150.5 14.0 %copy-start.17 = (f32[1,216,64]{1,2,0:T(8,128)}, f32[1,216,64]{1,2,0:T(8,128)S(1)}, u32[]{:S(2)}) copy-start(f32[1,216,64]{1,2,0:T(8,128)S(1)} %mul.81) | copy-start | bytes 165892
  164.5 8.8 %copy-start.25 = (f32[1,108,64]{1,2,0:T(8,128)}, f32[1,108,64]{1,2,0:T(8,128)S(1)}, u32[]{:S(2)}) copy-start(f32[1,108,64]{1,2,0:T(8,128)S(1)} %mul.78) | copy-start | bytes 82948
  165.2 84.0 %collective-permute-start.3 = (f32[1,324,64]{1,2,0:T(8,128)}, f32[1,324,64]{1,2,0:T(8,128)}, u32[]{:S(2)}, u32[]{:S(2)}) collective-permute-start(f32[1,324,64]{1,2,0:T(8,128)} %pad_maximum_fusion.9), channel_id=1, source_target_pairs={{1,0},{2,1},{3,2},{4,3},{5,4},{6,5},{7,6},{8,7},{9,8},{10,9},{11,1... | collective-permute-start | bytes 248840 | tf_op jit(solution)/shard_map/ppermute | solution.py:26
  167.1 82.1 %collective-permute-start.2 = (f32[1,324,64]{1,2,0:T(8,128)}, f32[1,324,64]{1,2,0:T(8,128)}, u32[]{:S(2)}, u32[]{:S(2)}) collective-permute-start(f32[1,324,64]{1,2,0:T(8,128)} %pad_maximum_fusion.9), channel_id=1, source_target_pairs={{0,1},{1,2},{2,3},{3,4},{4,5},{5,6},{6,7},{7,8},{8,9},{9,10},{10,1... | collective-permute-start | bytes 248840 | tf_op jit(solution)/shard_map/ppermute | solution.py:25
  207.6 5.4 %copy-start.12 = (f32[2,27,1,4,1,4,1,4]{5,4,3,2,1,0,7,6:T(1,128)S(1)}, f32[2,27,1,4,1,4,1,4]{5,4,3,2,1,0,7,6:T(1,128)}, u32[]{:S(2)}) copy-start(f32[2,27,1,4,1,4,1,4]{5,4,3,2,1,0,7,6:T(1,128)} %get-tuple-element.49) | copy-start | bytes 41476
  207.6 6.4 %copy-start.11 = (f32[2,27,1,4,1,4,1,4]{5,4,3,2,1,0,7,6:T(1,128)S(1)}, f32[2,27,1,4,1,4,1,4]{5,4,3,2,1,0,7,6:T(1,128)}, u32[]{:S(2)}) copy-start(f32[2,27,1,4,1,4,1,4]{5,4,3,2,1,0,7,6:T(1,128)} %get-tuple-element.43) | copy-start | bytes 41476
  207.6 7.4 %copy-start.10 = (f32[2,27,1,4,1,4,1,4]{5,4,3,2,1,0,7,6:T(1,128)S(1)}, f32[2,27,1,4,1,4,1,4]{5,4,3,2,1,0,7,6:T(1,128)}, u32[]{:S(2)}) copy-start(f32[2,27,1,4,1,4,1,4]{5,4,3,2,1,0,7,6:T(1,128)} %get-tuple-element.44) | copy-start | bytes 41476
  207.6 8.5 %copy-start.9 = (f32[2,27,1,4,1,4,1,4]{5,4,3,2,1,0,7,6:T(1,128)S(1)}, f32[2,27,1,4,1,4,1,4]{5,4,3,2,1,0,7,6:T(1,128)}, u32[]{:S(2)}) copy-start(f32[2,27,1,4,1,4,1,4]{5,4,3,2,1,0,7,6:T(1,128)} %get-tuple-element.45) | copy-start | bytes 41476
  207.6 9.5 %copy-start.8 = (f32[2,27,1,4,1,4,1,4]{5,4,3,2,1,0,7,6:T(1,128)S(1)}, f32[2,27,1,4,1,4,1,4]{5,4,3,2,1,0,7,6:T(1,128)}, u32[]{:S(2)}) copy-start(f32[2,27,1,4,1,4,1,4]{5,4,3,2,1,0,7,6:T(1,128)} %get-tuple-element.46) | copy-start | bytes 41476
  207.7 10.5 %copy-start.7 = (f32[2,27,1,4,1,4,1,4]{5,4,3,2,1,0,7,6:T(1,128)S(1)}, f32[2,27,1,4,1,4,1,4]{5,4,3,2,1,0,7,6:T(1,128)}, u32[]{:S(2)}) copy-start(f32[2,27,1,4,1,4,1,4]{5,4,3,2,1,0,7,6:T(1,128)} %get-tuple-element.47) | copy-start | bytes 41476
  213.0 24.4 %copy-start.5 = (f32[4,27,1,4,1,4,1,4]{5,4,3,2,1,0,7,6:T(1,128)S(1)}, f32[4,27,1,4,1,4,1,4]{5,4,3,2,1,0,7,6:T(1,128)}, u32[]{:S(2)}) copy-start(f32[4,27,1,4,1,4,1,4]{5,4,3,2,1,0,7,6:T(1,128)} %get-tuple-element.38) | copy-start | bytes 82948
  215.1 24.2 %copy-start.4 = (f32[4,27,1,4,1,4,1,4]{5,4,3,2,1,0,7,6:T(1,128)S(1)}, f32[4,27,1,4,1,4,1,4]{5,4,3,2,1,0,7,6:T(1,128)}, u32[]{:S(2)}) copy-start(f32[4,27,1,4,1,4,1,4]{5,4,3,2,1,0,7,6:T(1,128)} %get-tuple-element.39) | copy-start | bytes 82948
  217.1 23.0 %copy-start.3 = (f32[4,27,1,4,1,4,1,4]{5,4,3,2,1,0,7,6:T(1,128)S(1)}, f32[4,27,1,4,1,4,1,4]{5,4,3,2,1,0,7,6:T(1,128)}, u32[]{:S(2)}) copy-start(f32[4,27,1,4,1,4,1,4]{5,4,3,2,1,0,7,6:T(1,128)} %get-tuple-element.40) | copy-start | bytes 82948
  219.4 21.6 %copy-start.2 = (f32[4,27,1,4,1,4,1,4]{5,4,3,2,1,0,7,6:T(1,128)S(1)}, f32[4,27,1,4,1,4,1,4]{5,4,3,2,1,0,7,6:T(1,128)}, u32[]{:S(2)}) copy-start(f32[4,27,1,4,1,4,1,4]{5,4,3,2,1,0,7,6:T(1,128)} %get-tuple-element.34) | copy-start | bytes 82948
  241.9 7.4 %copy-start.18 = (f32[1,216,64]{1,2,0:T(8,128)S(1)}, f32[1,216,64]{1,2,0:T(8,128)}, u32[]{:S(2)}) copy-start(f32[1,216,64]{1,2,0:T(8,128)} %copy-done.17) | copy-start | bytes 165892
  241.9 7.3 %copy-start.26 = (f32[1,108,64]{1,2,0:T(8,128)S(1)}, f32[1,108,64]{1,2,0:T(8,128)}, u32[]{:S(2)}) copy-start(f32[1,108,64]{1,2,0:T(8,128)} %copy-done.25) | copy-start | bytes 82948
  241.9 10.0 %copy-start.37 = (f32[2,27,1,4,1,4,1,4]{1,7,5,3,0,6,4,2:T(4,128)S(1)}, f32[2,27,1,4,1,4,1,4]{1,7,5,3,0,6,4,2:T(4,128)}, u32[]{:S(2)}) copy-start(f32[2,27,1,4,1,4,1,4]{1,7,5,3,0,6,4,2:T(4,128)} %copy.422) | copy-start | bytes 41476
  241.9 10.0 %copy-start.55 = (pred[2]{0:T(512)(128)(4,1)S(1)}, pred[2]{0:T(512)(128)(4,1)}, u32[]{:S(2)}) copy-start(pred[2]{0:T(512)(128)(4,1)} %get-tuple-element.32) | copy-start | bytes 10
  241.9 10.1 %copy-start.36 = (f32[2,27,1,4,1,4,1,4]{1,7,5,3,0,6,4,2:T(4,128)S(1)}, f32[2,27,1,4,1,4,1,4]{1,7,5,3,0,6,4,2:T(4,128)}, u32[]{:S(2)}) copy-start(f32[2,27,1,4,1,4,1,4]{1,7,5,3,0,6,4,2:T(4,128)} %copy.421) | copy-start | bytes 41476
  241.9 10.1 %copy-start.53 = (pred[2]{0:T(512)(128)(4,1)S(1)}, pred[2]{0:T(512)(128)(4,1)}, u32[]{:S(2)}) copy-start(pred[2]{0:T(512)(128)(4,1)} %get-tuple-element.33) | copy-start | bytes 10
  248.1 4.1 %copy-start.35 = (f32[2,27,1,4,1,4,1,4]{1,7,5,3,0,6,4,2:T(4,128)S(1)}, f32[2,27,1,4,1,4,1,4]{1,7,5,3,0,6,4,2:T(4,128)}, u32[]{:S(2)}) copy-start(f32[2,27,1,4,1,4,1,4]{1,7,5,3,0,6,4,2:T(4,128)} %copy.420) | copy-start | bytes 41476
  248.1 4.1 %copy-start.51 = (pred[2]{0:T(512)(128)(4,1)S(1)}, pred[2]{0:T(512)(128)(4,1)}, u32[]{:S(2)}) copy-start(pred[2]{0:T(512)(128)(4,1)} %get-tuple-element.27) | copy-start | bytes 10
  248.1 4.2 %copy-start.34 = (f32[2,27,1,4,1,4,1,4]{1,7,5,3,0,6,4,2:T(4,128)S(1)}, f32[2,27,1,4,1,4,1,4]{1,7,5,3,0,6,4,2:T(4,128)}, u32[]{:S(2)}) copy-start(f32[2,27,1,4,1,4,1,4]{1,7,5,3,0,6,4,2:T(4,128)} %copy.419) | copy-start | bytes 41476
  248.1 4.2 %copy-start.49 = (pred[2]{0:T(512)(128)(4,1)S(1)}, pred[2]{0:T(512)(128)(4,1)}, u32[]{:S(2)}) copy-start(pred[2]{0:T(512)(128)(4,1)} %get-tuple-element.28) | copy-start | bytes 10
  248.1 4.4 %copy-start.33 = (f32[2,27,1,4,1,4,1,4]{1,7,5,3,0,6,4,2:T(4,128)S(1)}, f32[2,27,1,4,1,4,1,4]{1,7,5,3,0,6,4,2:T(4,128)}, u32[]{:S(2)}) copy-start(f32[2,27,1,4,1,4,1,4]{1,7,5,3,0,6,4,2:T(4,128)} %copy.418) | copy-start | bytes 41476
  248.1 4.4 %copy-start.48 = (pred[2]{0:T(512)(128)(4,1)S(1)}, pred[2]{0:T(512)(128)(4,1)}, u32[]{:S(2)}) copy-start(pred[2]{0:T(512)(128)(4,1)} %get-tuple-element.29) | copy-start | bytes 10
  248.1 4.5 %copy-start.32 = (f32[2,27,1,4,1,4,1,4]{1,7,5,3,0,6,4,2:T(4,128)S(1)}, f32[2,27,1,4,1,4,1,4]{1,7,5,3,0,6,4,2:T(4,128)}, u32[]{:S(2)}) copy-start(f32[2,27,1,4,1,4,1,4]{1,7,5,3,0,6,4,2:T(4,128)} %copy.417) | copy-start | bytes 41476
  248.1 4.5 %copy-start.47 = (pred[2]{0:T(512)(128)(4,1)S(1)}, pred[2]{0:T(512)(128)(4,1)}, u32[]{:S(2)}) copy-start(pred[2]{0:T(512)(128)(4,1)} %get-tuple-element.30) | copy-start | bytes 10
  248.2 4.6 %copy-start.31 = (f32[2,27,1,4,1,4,1,4]{1,7,5,3,0,6,4,2:T(4,128)S(1)}, f32[2,27,1,4,1,4,1,4]{1,7,5,3,0,6,4,2:T(4,128)}, u32[]{:S(2)}) copy-start(f32[2,27,1,4,1,4,1,4]{1,7,5,3,0,6,4,2:T(4,128)} %copy.416) | copy-start | bytes 41476
  248.2 4.6 %copy-start.46 = (pred[2]{0:T(512)(128)(4,1)S(1)}, pred[2]{0:T(512)(128)(4,1)}, u32[]{:S(2)}) copy-start(pred[2]{0:T(512)(128)(4,1)} %get-tuple-element.31) | copy-start | bytes 10
  248.2 4.7 %copy-start.30 = (f32[2,27,1,4,1,4,1,4]{1,7,5,3,0,6,4,2:T(4,128)S(1)}, f32[2,27,1,4,1,4,1,4]{1,7,5,3,0,6,4,2:T(4,128)}, u32[]{:S(2)}) copy-start(f32[2,27,1,4,1,4,1,4]{1,7,5,3,0,6,4,2:T(4,128)} %copy.415) | copy-start | bytes 41476
  248.2 4.7 %copy-start.45 = (pred[2]{0:T(512)(128)(4,1)S(1)}, pred[2]{0:T(512)(128)(4,1)}, u32[]{:S(2)}) copy-start(pred[2]{0:T(512)(128)(4,1)} %get-tuple-element.26) | copy-start | bytes 10
  253.1 4.6 %copy-start.24 = (f32[4,27,1,4,1,4,1,4]{1,7,5,3,0,6,4,2:T(4,128)S(1)}, f32[4,27,1,4,1,4,1,4]{1,7,5,3,0,6,4,2:T(4,128)}, u32[]{:S(2)}) copy-start(f32[4,27,1,4,1,4,1,4]{1,7,5,3,0,6,4,2:T(4,128)} %copy.430) | copy-start | bytes 82948
  253.1 4.6 %copy-start.60 = (pred[4]{0:T(512)(128)(4,1)S(1)}, pred[4]{0:T(512)(128)(4,1)}, u32[]{:S(2)}) copy-start(pred[4]{0:T(512)(128)(4,1)} %get-tuple-element.24) | copy-start | bytes 16
  253.3 4.6 %copy-start.23 = (f32[4,27,1,4,1,4,1,4]{1,7,5,3,0,6,4,2:T(4,128)S(1)}, f32[4,27,1,4,1,4,1,4]{1,7,5,3,0,6,4,2:T(4,128)}, u32[]{:S(2)}) copy-start(f32[4,27,1,4,1,4,1,4]{1,7,5,3,0,6,4,2:T(4,128)} %copy.429) | copy-start | bytes 82948
  253.3 4.6 %copy-start.59 = (pred[4]{0:T(512)(128)(4,1)S(1)}, pred[4]{0:T(512)(128)(4,1)}, u32[]{:S(2)}) copy-start(pred[4]{0:T(512)(128)(4,1)} %get-tuple-element.25) | copy-start | bytes 16
  253.4 4.6 %copy-start.22 = (f32[4,27,1,4,1,4,1,4]{1,7,5,3,0,6,4,2:T(4,128)S(1)}, f32[4,27,1,4,1,4,1,4]{1,7,5,3,0,6,4,2:T(4,128)}, u32[]{:S(2)}) copy-start(f32[4,27,1,4,1,4,1,4]{1,7,5,3,0,6,4,2:T(4,128)} %copy.428) | copy-start | bytes 82948
  253.4 4.6 %copy-start.58 = (pred[4]{0:T(512)(128)(4,1)S(1)}, pred[4]{0:T(512)(128)(4,1)}, u32[]{:S(2)}) copy-start(pred[4]{0:T(512)(128)(4,1)} %get-tuple-element.19) | copy-start | bytes 16
  253.5 4.7 %copy-start.21 = (f32[4,27,1,4,1,4,1,4]{1,7,5,3,0,6,4,2:T(4,128)S(1)}, f32[4,27,1,4,1,4,1,4]{1,7,5,3,0,6,4,2:T(4,128)}, u32[]{:S(2)}) copy-start(f32[4,27,1,4,1,4,1,4]{1,7,5,3,0,6,4,2:T(4,128)} %copy.427) | copy-start | bytes 82948
  253.5 4.7 %copy-start.57 = (pred[4]{0:T(512)(128)(4,1)S(1)}, pred[4]{0:T(512)(128)(4,1)}, u32[]{:S(2)}) copy-start(pred[4]{0:T(512)(128)(4,1)} %get-tuple-element.20) | copy-start | bytes 16
  255.6 2.9 %copy-start.20 = (f32[4,27,1,4,1,4,1,4]{1,7,5,3,0,6,4,2:T(4,128)S(1)}, f32[4,27,1,4,1,4,1,4]{1,7,5,3,0,6,4,2:T(4,128)}, u32[]{:S(2)}) copy-start(f32[4,27,1,4,1,4,1,4]{1,7,5,3,0,6,4,2:T(4,128)} %copy.426) | copy-start | bytes 82948
  255.6 2.9 %copy-start.56 = (pred[4]{0:T(512)(128)(4,1)S(1)}, pred[4]{0:T(512)(128)(4,1)}, u32[]{:S(2)}) copy-start(pred[4]{0:T(512)(128)(4,1)} %get-tuple-element.21) | copy-start | bytes 16
  255.6 3.0 %copy-start.54 = (pred[4]{0:T(512)(128)(4,1)S(1)}, pred[4]{0:T(512)(128)(4,1)}, u32[]{:S(2)}) copy-start(pred[4]{0:T(512)(128)(4,1)} %get-tuple-element.22) | copy-start | bytes 16
  (4 other events, 6.9 us)

commit v2 on v1

v2 whole, which is shorter than its diff:
```python
import functools

import jax
import jax.numpy as jnp
from jax import lax
from jax.experimental import pallas as pl
from jax.experimental.pallas import tpu as pltpu
from jax.sharding import PartitionSpec as P

SLOTS = 16
LANES = 128
MESH = pl.DeviceIdType.MESH


def forward(f, stride):
    out = list(f)
    for i in range(27):
        if i // stride % 3 == 0:
            lo, mid, hi = f[i], f[i + stride], f[i + 2 * stride]
            both = lo + hi
            out[i] = both + mid
            out[i + stride] = hi - lo
            out[i + 2 * stride] = both
    return out


def backward(m, stride):
    out = list(m)
    for i in range(27):
        if i // stride % 3 == 0:
            m0, m1, m2 = m[i], m[i + stride], m[i + 2 * stride]
            out[i] = 0.5 * (m2 - m1)
            out[i + stride] = m0 - m2
            out[i + 2 * stride] = 0.5 * (m1 + m2)
    return out


def collide_row(f, keep, rate_ref):
    for stride in (9, 3, 1):
        f = forward(f, stride)
    rho = f[0]
    scale = keep / rho
    mu = []
    for k in (9, 3, 1):
        v = f[k] * scale
        mu.append((None, v, 1.0 / 3.0 + v * v))
    for a in range(3):
        ta = rho if a == 0 else rho * mu[0][a]
        for b in range(3):
            tb = ta if b == 0 else ta * mu[1][b]
            for c in range(3):
                t = tb if c == 0 else tb * mu[2][c]
                i = 9 * a + 3 * b + c
                f[i] = f[i] - rate_ref[i : i + 1, :] * (f[i] - t)
    for stride in (9, 3, 1):
        f = backward(f, stride)
    return f


PACKS = (0, 8, 16, 20)
OUT_PACKS = (0, 8, 16, 19)


def pick_rows(v, rows):
    return jnp.take_along_axis(v, rows, axis=0, mode="promise_in_bounds")


def pick(v, idx):
    return jnp.take_along_axis(v, idx, axis=1, mode="promise_in_bounds")


def lbm_kernel(
    n, n_fine, n_mid, f_ref, rate_ref, raw_ref, out_ref,
    P, Q, R, G, snap, S, RV, T, keep_ref, tab_ref, PK, PR, M, MR, send_sem, recv_sem,
):
    me = lax.axis_index("blk")
    right, left = lax.rem(me + 1, n), lax.rem(me + n - 1, n)
    barrier = pltpu.get_barrier_semaphore()

    @pl.when(me > 0)
    def _():
        pl.semaphore_signal(barrier, inc=1, device_id=(left,), device_id_type=MESH)

    @pl.when(me < n - 1)
    def _():
        pl.semaphore_signal(barrier, inc=1, device_id=(right,), device_id_type=MESH)

    lane = lax.broadcasted_iota(jnp.int32, (8, LANES), 1)
    lane64 = lax.broadcasted_iota(jnp.int32, (64, LANES), 1)
    row64 = lax.broadcasted_iota(jnp.int32, (64, LANES), 0) % 8

    def copies(slot, src, dst):
        out = []
        for side, target in ((0, right), (1, left)):
            out.append(
                pltpu.make_async_remote_copy(
                    src_ref=src,
                    dst_ref=dst(side),
                    send_sem=send_sem.at[slot, side],
                    recv_sem=recv_sem.at[slot, side],
                    device_id=(target,),
                    device_id_type=MESH,
                )
            )
        return out

    def faces(slot):
        return slot, S.at[slot], lambda side: RV.at[slot, side]

    def send(slot, src, dst):
        up, down = copies(slot, src, dst)

        @pl.when(me < n - 1)
        def _():
            up.start()

        @pl.when(me > 0)
        def _():
            down.start()

    def receive(slot, src, dst):
        up, down = copies(slot, src, dst)

        @pl.when(me < n - 1)
        def _():
            up.wait_send()
            down.wait_recv()

        @pl.when(me > 0)
        def _():
            down.wait_send()
            up.wait_recv()

    def own(slot, axis):
        for d in range(2):
            idx, dev = tab_ref[4 * axis + 2 * d], tab_ref[4 * axis + 2 * d + 1]
            for j in range(9):
                G[d, j] = jnp.where(dev == 0, pick(S[slot, d, j], idx), G[d, j])

    def merge(slot, axis, d, j):
        idx, dev = tab_ref[4 * axis + 2 * d], tab_ref[4 * axis + 2 * d + 1]
        g = jnp.where(dev == -1, pick(RV[slot, 0, d, j], idx), G[d, j])
        return jnp.where(dev == 1, pick(RV[slot, 1, d, j], idx), g)

    def collide_at(x):
        at = pl.ds(pl.multiple_of(8 * x, 8), 8)
        f = collide_row([R[i, at, :] for i in range(27)], keep_ref[at, :], rate_ref)
        to = pl.ds(pl.multiple_of(8 * x + 8, 8), 8)
        for i in range(27):
            P[i, to, :] = f[i]

    def step_body(step, carry):
        @pl.loop(0, 2)
        def _(k):
            collide_at(7 * k)

        slot = 3 * step
        for j in range(9):
            S[slot, 0, j] = P[18 + j, 64:72, :]
            S[slot, 1, j] = P[j, 8:16, :]

        send(*faces(slot))

        @pl.loop(1, 7)
        def _(x):
            collide_at(x)

        for j in range(9):
            G[0, j] = P[18 + j, 8:16, :]
            G[1, j] = P[j, 64:72, :]
        own(slot, 0)
        receive(*faces(slot))
        for j in range(9):
            P[18 + j, 0:8, :] = merge(slot, 0, 0, j)
            P[j, 72:80, :] = merge(slot, 0, 1, j)

        slot = 3 * step + 1
        for j in range(9):
            a, c = j // 3, j % 3
            plus, minus, base = 9 * a + 6 + c, 9 * a + c, 8 * (2 - a)
            S[slot, 0, j] = P[plus, pl.ds(base + 7, 8, stride=8), :]
            S[slot, 1, j] = P[minus, pl.ds(base, 8, stride=8), :]
        send(*faces(slot))
        for j in range(9):
            a, c = j // 3, j % 3
            plus, rest, minus, base = 9 * a + 6 + c, 9 * a + 3 + c, 9 * a + c, 8 * (2 - a)
            G[0, j] = P[plus, pl.ds(base, 8, stride=8), :]
            G[1, j] = P[minus, pl.ds(base + 7, 8, stride=8), :]
            Q[rest] = P[rest, base : base + 64, :]
            Q[plus] = pltpu.roll(P[plus, base : base + 64, :], 1, 0)
            Q[minus] = pltpu.roll(P[minus, base : base + 64, :], 63, 0)
        own(slot, 1)
        receive(*faces(slot))
        for j in range(9):
            a, c = j // 3, j % 3
            Q[9 * a + 6 + c, pl.ds(0, 8, stride=8), :] = merge(slot, 1, 0, j)
            Q[9 * a + c, pl.ds(7, 8, stride=8), :] = merge(slot, 1, 1, j)

        slot = 3 * step + 2
        for j in range(9):
            plus, minus = 3 * j + 2, 3 * j
            hi = Q[plus, 56:64, :]
            lo = Q[minus, 0:8, :]
            for x in range(8):
                if x < 7:
                    v = pltpu.roll(Q[plus, 8 * x : 8 * x + 8, :], (16 * x + 16) % LANES, 1)
                    hi = jnp.where(lane // 16 == x, v, hi)
                if x > 0:
                    v = pltpu.roll(Q[minus, 8 * x : 8 * x + 8, :], 16 * x, 1)
                    lo = jnp.where(lane // 16 == x, v, lo)
            S[slot, 0, j] = hi
            S[slot, 1, j] = lo
        send(*faces(slot))
        for j in range(9):
            plus, rest, minus = 3 * j + 2, 3 * j + 1, 3 * j
            G[0, j] = jnp.zeros((8, LANES), jnp.float32)
            G[1, j] = jnp.zeros((8, LANES), jnp.float32)
            R[rest] = Q[rest]
            v = Q[plus]
            R[plus] = jnp.where(lane64 < 16, v, pltpu.roll(v, 16, 1))
            v = Q[minus]
            R[minus] = jnp.where(lane64 >= LANES - 16, v, pltpu.roll(v, LANES - 16, 1))
        own(slot, 2)
        receive(*faces(slot))
        take_low = (lane < 16) & (tab_ref[9] != 2)
        take_high = (lane >= LANES - 16) & (tab_ref[11] != 2)
        for j in range(9):
            low = merge(slot, 2, 0, j)
            high = merge(slot, 2, 1, j)
            for x in range(8):
                at = slice(8 * x, 8 * x + 8)
                v = low if x == 0 else pltpu.roll(low, (LANES - 16 * x) % LANES, 1)
                R[3 * j + 2, at, :] = jnp.where(take_low, v, R[3 * j + 2, at, :])
                v = high if x == 7 else pltpu.roll(high, (LANES - 16 - 16 * x) % LANES, 1)
                R[3 * j, at, :] = jnp.where(take_high, v, R[3 * j, at, :])

        @pl.when(step == 0)
        def _():
            snap[...] = R[...]

        @pl.when(step == 1)
        def _():
            for i in range(27):
                snap[i] = jnp.where(lane64 % SLOTS < n_fine + n_mid, R[i], snap[i])

        return carry

    for g, start in enumerate(PACKS):
        for c in range(4):
            at = slice(LANES * c, LANES * c + LANES)
            T[g, at, :] = f_ref[SLOTS * start : SLOTS * start + LANES, at].T
    for i in range(28):
        g = min(i // 8, 3)
        p = i - PACKS[g]
        acc = None
        for z in range(8):
            v = T[g, pl.ds(z, 64, stride=8), :]
            shift = (16 * (z - p)) % LANES
            v = pltpu.roll(v, shift, 1) if shift else v
            acc = v if z == 0 else jnp.where(lane64 // 16 == z, v, acc)
        if i < 27:
            R[i] = acc
        else:
            keep_ref[...] = 1.0 - acc

    half = lane % 64
    pack = (half // 8) * 16 + 8 + half % 8

    @pl.loop(0, 27)
    def _(i):
        for xl in range(4):
            lo = pick(R[i, 8 * xl : 8 * xl + 8, :], pack)
            hi = pick(R[i, 8 * xl + 32 : 8 * xl + 40, :], pack)
            PK[i, 8 * xl : 8 * xl + 8, :] = jnp.where(lane < 64, lo, hi)

    @pl.when((me == 0) | (me == n - 1))
    def _():
        pl.semaphore_wait(barrier, 1)

    @pl.when((me > 0) & (me < n - 1))
    def _():
        pl.semaphore_wait(barrier, 2)

    parents = (12, PK, lambda side: PR.at[side])
    send(*parents)

    def code(k):
        return jnp.broadcast_to(raw_ref[k : k + 1, :], (8, LANES))

    for k in range(6):
        c = code(k)
        tab_ref[2 * k] = (c & 15) + lane - lane % SLOTS
        tab_ref[2 * k + 1] = (c >> 4) - 1
    row = lax.broadcasted_iota(jnp.int32, (8, LANES), 0)
    z_at = lane >> 4
    c, o = code(6), code(7)
    dev = (c >> 4) - 1
    idx = (o >> 2) * 64 + ((o & 1) * 4 + (z_at >> 1)) * 8 + (c & 7)
    rows = ((o >> 1) & 1) * 4 + (row >> 1)
    has = dev != 2
    rim = has & ((row == 0) | (row == 7) | (z_at == 0) | (z_at == 7))
    receive(*parents)

    @pl.loop(0, 27)
    def _(i):
        for xl in range(4):
            at = slice(8 * xl, 8 * xl + 8)
            v = pick(PK[i, at, :], idx)
            v = jnp.where(dev == -1, pick(PR[0, i, at, :], idx), v)
            v = jnp.where(dev == 1, pick(PR[1, i, at, :], idx), v)
            v = pick_rows(v, rows)
            for x in (2 * xl, 2 * xl + 1):
                to = slice(8 * x, 8 * x + 8)
                R[i, to, :] = jnp.where(has if x in (0, 7) else rim, v, R[i, to, :])

    lax.fori_loop(0, 4, step_body, 0)

    even = row % 2 == 0
    first = z_at % 2 == 0

    @pl.loop(0, 27)
    def _(i):
        Q[i] = jnp.where(lane64 % SLOTS < n_fine, R[i], snap[i])
        sums = []
        for x in range(4):
            v = Q[i, 16 * x : 16 * x + 8, :] + Q[i, 16 * x + 8 : 16 * x + 16, :]
            v = v + pltpu.roll(v, 7, 0)
            sums.append(v + pltpu.roll(v, LANES - 16, 1))
        lo = jnp.where(even, sums[0], pltpu.roll(sums[1], 1, 0))
        hi = jnp.where(even, sums[2], pltpu.roll(sums[3], 1, 0))
        M[i] = jnp.where(first, lo, pltpu.roll(hi, 16, 1)) * 0.125

    means = (13, M, lambda side: MR.at[side])
    send(*means)
    idxs, devs = [], []
    for ox in range(2):
        near = jnp.where(z_at < 4, code(8 + 4 * ox), code(9 + 4 * ox))
        far = jnp.where(z_at < 4, code(10 + 4 * ox), code(11 + 4 * ox))
        c = jnp.where(row < 4, near, far)
        idxs.append((z_at & 3) * 32 + (c & 15))
        devs.append((c >> 4) - 1)
    receive(*means)

    @pl.loop(0, 27)
    def _(i):
        spread = [
            [pick_rows(v, 2 * (row & 3) + xa) for v in (M[i], MR[0, i], MR[1, i])] for xa in range(2)
        ]
        for x in range(8):
            ox, xa, xb = x // 4, x % 2, x // 2 % 2
            at = slice(8 * x, 8 * x + 8)
            idx, dev = idxs[ox] + 16 * xb, devs[ox]
            mine, low, high = spread[xa]
            v = jnp.where(dev == 0, pick(mine, idx), Q[i, at, :])
            v = jnp.where(dev == -1, pick(low, idx), v)
            R[i, at, :] = jnp.where(dev == 1, pick(high, idx), v)

    for g, start in enumerate(OUT_PACKS):
        for z in range(8):
            acc = None
            for p in range(8):
                i = start + p
                if i < 8 * g:
                    continue
                shift = (16 * (p - z)) % LANES
                v = pltpu.roll(R[i], shift, 1) if shift else R[i]
                acc = v if acc is None else jnp.where(lane64 // 16 == p, v, acc)
            T[g, pl.ds(z, 64, stride=8), :] = acc
        skip = 8 * g - start
        for c in range(4):
            at = slice(LANES * c, LANES * c + LANES)
            out_ref[SLOTS * 8 * g : SLOTS * (start + 8), at] = T[g, at, :].T[SLOTS * skip :, :]


def codes(table, count, base, place):
    group = table // count
    return jnp.where(table < 0, 48, 16 * (group - place + 1) + table - group * count + base)


def advance_all(
    f_coarse, f_mid, f_fine, solid_coarse, solid_mid, solid_fine, rates, faces_coarse, faces_mid,
    faces_fine, explode_mid, explode_fine, coalesce_coarse, coalesce_mid,
):
    n = lax.axis_size("blk")
    place = lax.axis_index("blk")
    n2, n1, n0 = f_fine.shape[0], f_mid.shape[0], f_coarse.shape[0]
    assert n2 == 8 and n1 + n0 <= 8
    spare = SLOTS - n0 - n1 - n2

    f_all = jnp.concatenate([f_fine, f_mid, f_coarse, jnp.ones((spare, 27, 512), jnp.float32)])
    solid = jnp.concatenate([solid_fine, solid_mid, solid_coarse, jnp.zeros((spare, 512), jnp.float32)])
    f_all = jnp.concatenate([f_all, solid[:, None, :]], axis=1)
    f_all = f_all.transpose(1, 0, 2).reshape(28 * SLOTS, 512)

    faces = jnp.concatenate([
        codes(faces_fine, n2, 0, place),
        codes(faces_mid, n1, n2, place),
        codes(faces_coarse, n0, n2 + n1, place),
        jnp.full((spare, 6), 48, jnp.int32),
    ])
    parent = jnp.concatenate([
        codes(explode_fine[:, 0], n1, 0, place),
        codes(explode_mid[:, 0], n0, n1, place),
        jnp.full((n0 + spare,), 48, jnp.int32),
    ])
    octant = jnp.concatenate([explode_fine[:, 1], explode_mid[:, 1], jnp.zeros((n0 + spare,), jnp.int32)])
    child = jnp.concatenate([
        jnp.full((n2, 8), 48, jnp.int32),
        codes(coalesce_mid, n2, 0, place),
        codes(coalesce_coarse, n1, n2, place),
        jnp.full((spare, 8), 48, jnp.int32),
    ])
    raw = jnp.concatenate([faces, parent[:, None], octant[:, None], child], axis=1).T
    raw = jnp.tile(raw, (1, 8))

    slot = jnp.arange(LANES)[None, :] % SLOTS
    r0, r1, r2 = rates[0][:, None], rates[1][:, None], rates[2][:, None]
    rate = jnp.where(slot < n2, r2, jnp.where(slot < n2 + n1, r1, r0))

    vmem = pl.BlockSpec(memory_space=pltpu.VMEM)
    f32 = jnp.float32
    out = pl.pallas_call(
        functools.partial(lbm_kernel, n, n2, n1),
        out_shape=jax.ShapeDtypeStruct((27 * SLOTS, 512), f32),
        in_specs=[vmem] * 3,
        out_specs=vmem,
        scratch_shapes=[
            pltpu.VMEM((27, 80, LANES), f32),
            pltpu.VMEM((27, 64, LANES), f32),
            pltpu.VMEM((27, 64, LANES), f32),
            pltpu.VMEM((2, 9, 8, LANES), f32),
            pltpu.VMEM((27, 64, LANES), f32),
            pltpu.VMEM((12, 2, 9, 8, LANES), f32),
            pltpu.VMEM((12, 2, 2, 9, 8, LANES), f32),
            pltpu.VMEM((4, 512, LANES), f32),
            pltpu.VMEM((64, LANES), f32),
            pltpu.VMEM((12, 8, LANES), jnp.int32),
            pltpu.VMEM((27, 32, LANES), f32),
            pltpu.VMEM((2, 27, 32, LANES), f32),
            pltpu.VMEM((27, 8, LANES), f32),
            pltpu.VMEM((2, 27, 8, LANES), f32),
            pltpu.SemaphoreType.DMA((14, 2)),
            pltpu.SemaphoreType.DMA((14, 2)),
        ],
        compiler_params=pltpu.CompilerParams(
            collective_id=0, has_side_effects=True, vmem_limit_bytes=40 * 1024 * 1024
        ),
    )(f_all, rate, raw)
    out = out.reshape(27, SLOTS, 512)
    parts = [out[:, n2 + n1 : n2 + n1 + n0], out[:, n2 : n2 + n1], out[:, :n2]]
    return tuple(p.transpose(1, 0, 2) for p in parts)


def solution(mesh):
    row, table = P("blk", None, None), P("blk", None)
    return jax.shard_map(
        advance_all,
        mesh=mesh,
        in_specs=(row,) * 3 + (table,) * 3 + (P(),) + (table,) * 7,
        out_specs=(row,) * 3,
        check_vma=False,
    )
```

time: 265 us -> 92.8 us (0.35)
  local copies, waits for them, and re-layouts: 141 us -> 4.91 us
  other arithmetic: 39.1 us -> 7.16 us
  Pallas kernels: 63.9 us -> 78.7 us
  starting transfers between devices: 14.7 us -> 0 us
    unnamed x154 -> x4, local copies, waits for them, and re-layouts: 41.3 us -> 0.01 us
    slice x33 -> x0, local copies, waits for them, and re-layouts: 40.6 us -> none  [the longest x7 21.1 us: advance_all(): return (back[:fine], back[fine:mid], back[mid:mid + counts[2]])]
    reshape x10 -> x0, local copies, waits for them, and re-layouts: 29.7 us -> none  [the longest x2 18.9 us: assemble(): grid = parent.reshape(count, 27, 2, half, 2, half, 2, half)]
    reduce_sum x2 -> x0, other arithmetic: 16.7 us -> none  [restrict(): return (jnp.sum(grid, axis=(3, 5, 7)) * 0.125).reshape(count, 27, half ** 3)]
    pallas_call x1, Pallas kernels: 63.9 us -> 78.7 us  [advance_all(): pl.pallas_call(functools.partial(lbm_kernel, n, n2, n1), out_shape=jax.Sh...]
    ppermute x4 -> x0, starting transfers between devices: 14.7 us -> none  [the longest x2 10.2 us: padded(): before = lax.ppermute(last, axis, up)]
    concatenate x8 -> x3, local copies, waits for them, and re-layouts: 9.27 us -> 0.23 us  [the longest x1 0.08 us: advance_all(): jnp.concatenate([codes(faces_fine, n2, 0, place), codes(faces_mid, n1, n2...]
    gather x8 -> x0, local copies, waits for them, and re-layouts: 5.4 us -> none  [the longest x4 3.85 us: lookup(): return table[slots]]
  transfers between devices with their start and end apart: 4 -> 0, of which waited for: 0 -> 0; matrix products, arithmetic and copies ran while one was open for 36% -> 0% of each run, Pallas kernels for 0% -> 0%
where the time goes in v2:
time: 92.8 us; the launch traced here: 91.5 us
  Pallas kernels  78.7 us (85%)
  other arithmetic  7.16 us (8%)
  local copies, waits for them, and re-layouts  4.91 us (5%)
    pallas_call x1, Pallas kernels, advance_all(): pl.pallas_call(functools.partial(lbm_kernel, n, n2, n1), out_shape=jax.Sh...  78.7 us
    select_n x7, other arithmetic, codes(): jnp.where(table < 0, 48, 16 * (group - place + 1) + table - group * count...  4.87 us
    transpose x3, local copies, waits for them, and re-layouts, advance_all(): return tuple((p.transpose(1, 0, 2) for p in parts))  2.2 us

profile of v2, /device:TPU:23, one launch (start us, length us, event | category | flops | bytes accessed | tf_op | source)
XLA Modules:
  0.0 91.5 jit_solution(16007244876554272356)
XLA Ops:
  0.6 0.0 copy-start
  0.6 0.7 slice_bitcast_fusion.3
  1.4 0.7 compare_select_fusion.1
  2.1 0.7 slice_bitcast_fusion.4
  2.7 0.7 compare_select_fusion
  3.4 0.1 pad.25.clone
  3.5 0.1 add_bitcast_fusion.1
  3.6 0.7 add_select_fusion.5
  4.3 0.7 add_select_fusion.4
  5.0 0.8 slice_bitcast_fusion.7
  5.8 0.7 add_select_fusion.3
  6.5 0.7 subtract_select_fusion.1
  7.2 0.1 copy.17
  7.3 0.1 copy.18
  7.4 0.7 subtract_select_fusion
  8.1 0.1 copy.20
  8.2 0.1 add_bitcast_fusion
  8.3 0.1 select_select_fusion.rate_ref
  8.3 0.1 pad.20.clone
  8.4 0.0 copy-start.1
  8.4 0.9 maximum_bitcast_fusion
  9.3 0.1 tile.10.raw_ref
  9.4 0.0 copy-done
  9.4 0.0 copy-done.1
  9.4 1.2 %pad_maximum_fusion = f32[16,28,512]{2,0,1:T(8,128)S(1)} fusion(f32[16,1,512]{2,0,1:T(8,128)S(1)} %maximum_bitcast_fusion, f32[2,27,512]{2,0,1:T(2,128)S(1)} %copy-done.1, f32[4,27,512]{2,0,1:T(4,128)S(1)} %copy-done, f32[8,27,512]{2,0,1:T(8,128)} %param.16, f32[16,28]{0,1:T(8,128)S(1)} %pad.20.clone), kind=kLoop, calls=%fused_computation | loop fusion | flops 917504 | bytes 1726208 | tf_op jit(solution)/shard_map/concatenate | solution.py:392
  10.6 78.7 %shard_map.157 = f32[432,512]{1,0:T(8,128)S(1)} custom-call(f32[448,512]{1,0:T(8,128)S(1)} %bitcast.62, f32[27,128]{1,0:T(8,128)S(1)} %select_select_fusion.rate_ref, s32[16,128]{1,0:T(8,128)S(1)} %tile.10.raw_ref), custom_call_target="tpu_custom_call" | custom-call | tf_op jit(solution)/shard_map/pallas_call | solution.py:422
  89.3 0.7 slice_bitcast_fusion.2
  90.0 0.7 slice_bitcast_fusion.1
  90.7 0.8 slice_bitcast_fusion
  (10 shorter events, 0.0 us)
Async XLA Ops:
  0.6 8.7 %copy-start = (f32[4,27,512]{2,0,1:T(4,128)S(1)}, f32[4,27,512]{2,0,1:T(4,128)}, u32[]{:S(2)}) copy-start(f32[4,27,512]{2,0,1:T(4,128)} %param.15) | copy-start | bytes 663556
  8.4 1.0 %copy-start.1 = (f32[2,27,512]{2,0,1:T(2,128)S(1)}, f32[2,27,512]{2,0,1:T(2,128)}, u32[]{:S(2)}) copy-start(f32[2,27,512]{2,0,1:T(2,128)} %param.14) | copy-start | bytes 331780

commit v3 on v2

--- a/solution.py
+++ b/solution.py
@@ -70,7 +70,7 @@
 
 
 def lbm_kernel(
-    n, n_fine, n_mid, f_ref, rate_ref, raw_ref, out_ref,
+    n, n_fine, n_mid, n_coarse, f_ref, rate_ref, raw_ref, out_ref,
     P, Q, R, G, snap, S, RV, T, keep_ref, tab_ref, PK, PR, M, MR, send_sem, recv_sem,
 ):
     me = lax.axis_index("blk")
@@ -245,81 +245,100 @@
 
         return carry
 
+    def swap(vs):
+        for s in (1, 2, 4):
+            low, new = (lane // 16) & s == 0, list(vs)
+            for k in range(8):
+                if k & s == 0:
+                    a, b = vs[k], vs[k + s]
+                    new[k] = jnp.where(low, a, pltpu.roll(b, 16 * s, 1))
+                    new[k + s] = jnp.where(low, pltpu.roll(a, LANES - 16 * s, 1), b)
+            vs = new
+        return vs
+
+    def part(slot, src, dst, g):
+        at = pl.ds(8 * g, min(8, 27 - 8 * g))
+        return slot + g, src.at[at], lambda side: dst.at[side, at]
+
+    half = lane % 64
+    pack = (half // 8) * 16 + 8 + half % 8
     for g, start in enumerate(PACKS):
         for c in range(4):
             at = slice(LANES * c, LANES * c + LANES)
             T[g, at, :] = f_ref[SLOTS * start : SLOTS * start + LANES, at].T
-    for i in range(28):
-        g = min(i // 8, 3)
-        p = i - PACKS[g]
-        acc = None
-        for z in range(8):
-            v = T[g, pl.ds(z, 64, stride=8), :]
-            shift = (16 * (z - p)) % LANES
-            v = pltpu.roll(v, shift, 1) if shift else v
-            acc = v if z == 0 else jnp.where(lane64 // 16 == z, v, acc)
-        if i < 27:
-            R[i] = acc
-        else:
-            keep_ref[...] = 1.0 - acc
-
-    half = lane % 64
-    pack = (half // 8) * 16 + 8 + half % 8
-
-    @pl.loop(0, 27)
-    def _(i):
-        for xl in range(4):
-            lo = pick(R[i, 8 * xl : 8 * xl + 8, :], pack)
-            hi = pick(R[i, 8 * xl + 32 : 8 * xl + 40, :], pack)
-            PK[i, 8 * xl : 8 * xl + 8, :] = jnp.where(lane < 64, lo, hi)
-
-    @pl.when((me == 0) | (me == n - 1))
-    def _():
-        pl.semaphore_wait(barrier, 1)
-
-    @pl.when((me > 0) & (me < n - 1))
-    def _():
-        pl.semaphore_wait(barrier, 2)
-
-    parents = (12, PK, lambda side: PR.at[side])
-    send(*parents)
-
-    def code(k):
+        for x in range(8):
+            vs = swap([T[g, pl.ds(64 * x + z, 8, stride=8), :] for z in range(8)])
+            at = slice(8 * x, 8 * x + 8)
+            for p in range(8):
+                if 8 * g <= start + p < 27:
+                    R[start + p, at, :] = vs[p]
+                elif start + p == 27:
+                    keep_ref[at, :] = 1.0 - vs[p]
+        for i in range(8 * g, min(8 * g + 8, 27)):
+            for xl in range(4):
+                lo = pick(R[i, 8 * xl : 8 * xl + 8, :], pack)
+                hi = pick(R[i, 8 * xl + 32 : 8 * xl + 40, :], pack)
+                PK[i, 8 * xl : 8 * xl + 8, :] = jnp.where(lane < 64, lo, hi)
+        if g == 0:
+
+            @pl.when((me == 0) | (me == n - 1))
+            def _():
+                pl.semaphore_wait(barrier, 1)
+
+            @pl.when((me > 0) & (me < n - 1))
+            def _():
+                pl.semaphore_wait(barrier, 2)
+
+        send(*part(12, PK, PR, g))
+
+    slot_at = lane % SLOTS
+
+    def raw(k):
         return jnp.broadcast_to(raw_ref[k : k + 1, :], (8, LANES))
 
+    def by_level(values):
+        return jnp.where(
+            slot_at < n_fine, values[0], jnp.where(slot_at < n_fine + n_mid, values[1], values[2])
+        )
+
+    def code(v, counts, bases):
+        group = by_level([v >> (k.bit_length() - 1) for k in counts])
+        local = by_level([(v & (k - 1)) + b for k, b in zip(counts, bases)])
+        return local, jnp.where(v < 0, 2, group - me)
+
     for k in range(6):
-        c = code(k)
-        tab_ref[2 * k] = (c & 15) + lane - lane % SLOTS
-        tab_ref[2 * k + 1] = (c >> 4) - 1
+        local, dev = code(raw(k), (n_fine, n_mid, n_coarse), (0, n_fine, n_fine + n_mid))
+        tab_ref[2 * k] = local + lane - slot_at
+        tab_ref[2 * k + 1] = dev
     row = lax.broadcasted_iota(jnp.int32, (8, LANES), 0)
     z_at = lane >> 4
-    c, o = code(6), code(7)
-    dev = (c >> 4) - 1
-    idx = (o >> 2) * 64 + ((o & 1) * 4 + (z_at >> 1)) * 8 + (c & 7)
-    rows = ((o >> 1) & 1) * 4 + (row >> 1)
+    local, dev = code(raw(6), (n_mid, n_coarse, n_coarse), (0, n_mid, 0))
+    o = raw(7)
+    idx = (o & 4) * 16 + ((o & 1) * 4 + (z_at >> 1)) * 8 + local
+    rows = (o & 2) * 2 + (row >> 1)
     has = dev != 2
     rim = has & ((row == 0) | (row == 7) | (z_at == 0) | (z_at == 7))
-    receive(*parents)
-
-    @pl.loop(0, 27)
-    def _(i):
-        for xl in range(4):
-            at = slice(8 * xl, 8 * xl + 8)
-            v = pick(PK[i, at, :], idx)
-            v = jnp.where(dev == -1, pick(PR[0, i, at, :], idx), v)
-            v = jnp.where(dev == 1, pick(PR[1, i, at, :], idx), v)
-            v = pick_rows(v, rows)
-            for x in (2 * xl, 2 * xl + 1):
-                to = slice(8 * x, 8 * x + 8)
-                R[i, to, :] = jnp.where(has if x in (0, 7) else rim, v, R[i, to, :])
+    for g in range(4):
+        receive(*part(12, PK, PR, g))
+
+        @pl.loop(8 * g, min(8 * g + 8, 27))
+        def _(i):
+            for xl in range(4):
+                at = slice(8 * xl, 8 * xl + 8)
+                v = pick(PK[i, at, :], idx)
+                v = jnp.where(dev == -1, pick(PR[0, i, at, :], idx), v)
+                v = jnp.where(dev == 1, pick(PR[1, i, at, :], idx), v)
+                v = pick_rows(v, rows)
+                for x in (2 * xl, 2 * xl + 1):
+                    to = slice(8 * x, 8 * x + 8)
+                    R[i, to, :] = jnp.where(has if x in (0, 7) else rim, v, R[i, to, :])
 
     lax.fori_loop(0, 4, step_body, 0)
 
     even = row % 2 == 0
     first = z_at % 2 == 0
 
-    @pl.loop(0, 27)
-    def _(i):
+    def mean(i):
         Q[i] = jnp.where(lane64 % SLOTS < n_fine, R[i], snap[i])
         sums = []
         for x in range(4):
@@ -330,19 +349,19 @@
         hi = jnp.where(even, sums[2], pltpu.roll(sums[3], 1, 0))
         M[i] = jnp.where(first, lo, pltpu.roll(hi, 16, 1)) * 0.125
 
-    means = (13, M, lambda side: MR.at[side])
-    send(*means)
+    for g in range(4):
+        pl.loop(8 * g, min(8 * g + 8, 27))(mean)
+        send(*part(16, M, MR, g))
+
     idxs, devs = [], []
     for ox in range(2):
-        near = jnp.where(z_at < 4, code(8 + 4 * ox), code(9 + 4 * ox))
-        far = jnp.where(z_at < 4, code(10 + 4 * ox), code(11 + 4 * ox))
-        c = jnp.where(row < 4, near, far)
-        idxs.append((z_at & 3) * 32 + (c & 15))
-        devs.append((c >> 4) - 1)
-    receive(*means)
-
-    @pl.loop(0, 27)
-    def _(i):
+        near = jnp.where(z_at < 4, raw(8 + 4 * ox), raw(9 + 4 * ox))
+        far = jnp.where(z_at < 4, raw(10 + 4 * ox), raw(11 + 4 * ox))
+        local, dev = code(jnp.where(row < 4, near, far), (n_fine, n_fine, n_mid), (0, 0, n_fine))
+        idxs.append((z_at & 3) * 32 + local)
+        devs.append(dev)
+
+    def take_means(i):
         spread = [
             [pick_rows(v, 2 * (row & 3) + xa) for v in (M[i], MR[0, i], MR[1, i])] for xa in range(2)
         ]
@@ -356,25 +375,16 @@
             R[i, at, :] = jnp.where(dev == 1, pick(high, idx), v)
 
     for g, start in enumerate(OUT_PACKS):
-        for z in range(8):
-            acc = None
-            for p in range(8):
-                i = start + p
-                if i < 8 * g:
-                    continue
-                shift = (16 * (p - z)) % LANES
-                v = pltpu.roll(R[i], shift, 1) if shift else R[i]
-                acc = v if acc is None else jnp.where(lane64 // 16 == p, v, acc)
-            T[g, pl.ds(z, 64, stride=8), :] = acc
+        receive(*part(16, M, MR, g))
+        pl.loop(8 * g, min(8 * g + 8, 27))(take_means)
+        for x in range(8):
+            vs = swap([R[start + p, 8 * x : 8 * x + 8, :] for p in range(8)])
+            for z in range(8):
+                T[g, pl.ds(64 * x + z, 8, stride=8), :] = vs[z]
         skip = 8 * g - start
         for c in range(4):
             at = slice(LANES * c, LANES * c + LANES)
             out_ref[SLOTS * 8 * g : SLOTS * (start + 8), at] = T[g, at, :].T[SLOTS * skip :, :]
-
-
-def codes(table, count, base, place):
-    group = table // count
-    return jnp.where(table < 0, 48, 16 * (group - place + 1) + table - group * count + base)
 
 
 def advance_all(
@@ -382,9 +392,9 @@
     faces_fine, explode_mid, explode_fine, coalesce_coarse, coalesce_mid,
 ):
     n = lax.axis_size("blk")
-    place = lax.axis_index("blk")
     n2, n1, n0 = f_fine.shape[0], f_mid.shape[0], f_coarse.shape[0]
     assert n2 == 8 and n1 + n0 <= 8
+    assert all(k & (k - 1) == 0 for k in (n0, n1, n2))
     spare = SLOTS - n0 - n1 - n2
 
     f_all = jnp.concatenate([f_fine, f_mid, f_coarse, jnp.ones((spare, 27, 512), jnp.float32)])
@@ -392,26 +402,13 @@
     f_all = jnp.concatenate([f_all, solid[:, None, :]], axis=1)
     f_all = f_all.transpose(1, 0, 2).reshape(28 * SLOTS, 512)
 
-    faces = jnp.concatenate([
-        codes(faces_fine, n2, 0, place),
-        codes(faces_mid, n1, n2, place),
-        codes(faces_coarse, n0, n2 + n1, place),
-        jnp.full((spare, 6), 48, jnp.int32),
+    raw = jnp.concatenate([
+        jnp.concatenate([faces_fine, explode_fine, jnp.full((n2, 8), -1, jnp.int32)], axis=1),
+        jnp.concatenate([faces_mid, explode_mid, coalesce_mid], axis=1),
+        jnp.concatenate([faces_coarse, jnp.full((n0, 2), -1, jnp.int32), coalesce_coarse], axis=1),
+        jnp.full((spare, 16), -1, jnp.int32),
     ])
-    parent = jnp.concatenate([
-        codes(explode_fine[:, 0], n1, 0, place),
-        codes(explode_mid[:, 0], n0, n1, place),
-        jnp.full((n0 + spare,), 48, jnp.int32),
-    ])
-    octant = jnp.concatenate([explode_fine[:, 1], explode_mid[:, 1], jnp.zeros((n0 + spare,), jnp.int32)])
-    child = jnp.concatenate([
-        jnp.full((n2, 8), 48, jnp.int32),
-        codes(coalesce_mid, n2, 0, place),
-        codes(coalesce_coarse, n1, n2, place),
-        jnp.full((spare, 8), 48, jnp.int32),
-    ])
-    raw = jnp.concatenate([faces, parent[:, None], octant[:, None], child], axis=1).T
-    raw = jnp.tile(raw, (1, 8))
+    raw = jnp.tile(raw.T, (1, 8))
 
     slot = jnp.arange(LANES)[None, :] % SLOTS
     r0, r1, r2 = rates[0][:, None], rates[1][:, None], rates[2][:, None]
@@ -420,7 +417,7 @@
     vmem = pl.BlockSpec(memory_space=pltpu.VMEM)
     f32 = jnp.float32
     out = pl.pallas_call(
-        functools.partial(lbm_kernel, n, n2, n1),
+        functools.partial(lbm_kernel, n, n2, n1, n0),
         out_shape=jax.ShapeDtypeStruct((27 * SLOTS, 512), f32),
         in_specs=[vmem] * 3,
         out_specs=vmem,
@@ -439,8 +436,8 @@
             pltpu.VMEM((2, 27, 32, LANES), f32),
             pltpu.VMEM((27, 8, LANES), f32),
             pltpu.VMEM((2, 27, 8, LANES), f32),
-            pltpu.SemaphoreType.DMA((14, 2)),
-            pltpu.SemaphoreType.DMA((14, 2)),
+            pltpu.SemaphoreType.DMA((20, 2)),
+            pltpu.SemaphoreType.DMA((20, 2)),
         ],
         compiler_params=pltpu.CompilerParams(
             collective_id=0, has_side_effects=True, vmem_limit_bytes=40 * 1024 * 1024

time: 92.8 us -> 83 us (0.89)
  Pallas kernels: 78.7 us -> 71.9 us
  other arithmetic: 7.16 us -> 4.42 us
    pallas_call x1, Pallas kernels: 78.7 us -> 71.9 us  [advance_all(): pl.pallas_call(functools.partial(lbm_kernel, n, n2, n1, n0), out_shape=ja...]
    select_n x7 -> x0, other arithmetic: 4.87 us -> none  [codes(): jnp.where(table < 0, 48, 16 * (group - place + 1) + table - group * count...]
    concatenate x1 -> x2, other arithmetic: 0.01 us -> 1.54 us  [the longest x1 0.77 us: advance_all(): jnp.concatenate([faces_mid, explode_mid, coalesce_mid], axis=1)]
    unnamed x4 -> x6, local copies, waits for them, and re-layouts: 0.01 us -> 1.54 us
    squeeze x2 -> x0, local copies, waits for them, and re-layouts: 1.41 us -> none  [the longest x1 0.72 us: advance_all(): explode_mid[:, 1]]
where the time goes in v3:
time: 83 us; the launch traced here: 82.1 us
  Pallas kernels  71.9 us (87%)
  local copies, waits for them, and re-layouts  5.03 us (6%)
  other arithmetic  4.42 us (5%)
    pallas_call x1, Pallas kernels, advance_all(): pl.pallas_call(functools.partial(lbm_kernel, n, n2, n1, n0), out_shape=ja...  71.9 us
    transpose x3, local copies, waits for them, and re-layouts, advance_all(): return tuple((p.transpose(1, 0, 2) for p in parts))  2.2 us

profile of v3, /device:TPU:23, one launch (start us, length us, event | category | flops | bytes accessed | tf_op | source)
XLA Modules:
  0.0 82.1 jit_solution(14812664369667747134)
XLA Ops:
  0.6 0.0 copy-start
  0.7 0.1 pad.20.clone
  0.7 0.1 fusion
  0.8 0.8 pad_add_fusion.1
  1.6 0.8 slice_bitcast_fusion.5
  2.4 0.8 copy.18
  3.1 0.8 pad_add_fusion
  3.9 0.8 copy.17
  4.7 0.1 copy.19
  4.8 0.1 copy.20
  4.9 0.8 add_bitcast_fusion
  5.6 0.1 select_select_fusion.rate_ref
  5.7 0.1 pad.15.clone
  5.8 0.0 copy-start.1
  5.8 0.9 %maximum_bitcast_fusion = f32[16,1,512]{2,0,1:T(8,128)S(1)} fusion(f32[2,512]{1,0:T(2,128)} %param.17, f32[4,512]{1,0:T(4,128)} %param.18, f32[8,512]{1,0:T(8,128)} %param.19, f32[16]{0:T(128)S(1)} %pad.20.clone), kind=kLoop, calls=%fused_computation.4 | loop fusion | flops 24576 | bytes 61504 | tf_op jit(solution)/shard_map/broadcast_in_dim | solution.py:402
  6.6 0.1 tile.10.raw_ref
  6.7 0.0 copy-done
  6.7 0.0 copy-done.1
  6.7 1.2 %pad_maximum_fusion = f32[16,28,512]{2,0,1:T(8,128)S(1)} fusion(f32[16,1,512]{2,0,1:T(8,128)S(1)} %maximum_bitcast_fusion, f32[2,27,512]{2,0,1:T(2,128)S(1)} %copy-done.1, f32[4,27,512]{2,0,1:T(4,128)S(1)} %copy-done, f32[8,27,512]{2,0,1:T(8,128)} %param.16, f32[16,28]{0,1:T(8,128)S(1)} %pad.15.clone), kind=kLoop, calls=%fused_computation | loop fusion | flops 917504 | bytes 1726208 | tf_op jit(solution)/shard_map/concatenate | solution.py:402
  7.9 71.9 %shard_map.157 = f32[432,512]{1,0:T(8,128)S(1)} custom-call(f32[448,512]{1,0:T(8,128)S(1)} %bitcast.20, f32[27,128]{1,0:T(8,128)S(1)} %select_select_fusion.rate_ref, s32[16,128]{1,0:T(8,128)S(1)} %tile.10.raw_ref), custom_call_target="tpu_custom_call" | custom-call | tf_op jit(solution)/shard_map/pallas_call | solution.py:419
  79.9 0.7 slice_bitcast_fusion.2
  80.6 0.7 slice_bitcast_fusion.1
  81.3 0.8 slice_bitcast_fusion
  (6 shorter events, 0.0 us)
Async XLA Ops:
  0.6 6.1 %copy-start = (f32[4,27,512]{2,0,1:T(4,128)S(1)}, f32[4,27,512]{2,0,1:T(4,128)}, u32[]{:S(2)}) copy-start(f32[4,27,512]{2,0,1:T(4,128)} %param.15) | copy-start | bytes 663556
  5.8 1.0 %copy-start.1 = (f32[2,27,512]{2,0,1:T(2,128)S(1)}, f32[2,27,512]{2,0,1:T(2,128)}, u32[]{:S(2)}) copy-start(f32[2,27,512]{2,0,1:T(2,128)} %param.14) | copy-start | bytes 331780
